TPU v7x, 32 devices: a whole 2x2x4 slice. The times are simulated.
32 devices in a mesh: dp: 8 (over z, y), head: 4 (over x, core).
Axes of the slice: x: 2, y: 2, z: 4, core: 2. Of those that a mesh axis runs over, the one named last changes fastest.
Arguments:
- tokens: bfloat16 [131072, 512], P(('dp', 'head')), may hold values from -6 to 6
- lengths: int32 [128], P('dp'), may hold values from 512 to 1024, as said below
- feature_proj: float32 [8, 64, 128], replicated, may hold values from -0.75 to 0.75
- first_gain: bfloat16 [512], P(('dp', 'head')), may hold values from 0.5 to 1.5
- query_weight: bfloat16 [512, 512], P(('dp', 'head')), may hold values from -0.25 to 0.25
- key_weight: bfloat16 [512, 512], P(('dp', 'head')), may hold values from -0.25 to 0.25
- value_weight: bfloat16 [512, 512], P(('dp', 'head')), may hold values from -0.25 to 0.25
- gate_weight: bfloat16 [512, 8], P(('dp', 'head')), may hold values from -0.25 to 0.25
- gate_bias: float32 [8], replicated, may hold values from -1 to 7
- output_weight: bfloat16 [512, 512], P(('dp', 'head')), may hold values from -1 to 1
- second_gain: bfloat16 [512], P(('dp', 'head')), may hold values from 0.5 to 1.5
- up_weight: bfloat16 [512, 2048], P(('dp', 'head')), may hold values from -0.25 to 0.25
- down_weight: bfloat16 [2048, 512], P(('dp', 'head')), may hold values from -0.125 to 0.125
- cotangent: bfloat16 [131072, 512], P(('dp', 'head')), may hold values from -6 to 6
Outputs:
- mixed: bfloat16 [131072, 512], P(('dp', 'head'))
- grad_tokens: float32 [131072, 512], P(('dp', 'head'))
- grad_first_gain: float32 [512], P(('dp', 'head'))
- grad_query: float32 [512, 512], P(('dp', 'head'))
- grad_key: float32 [512, 512], P(('dp', 'head'))
- grad_value: float32 [512, 512], P(('dp', 'head'))
- grad_gate_weight: float32 [512, 8], P(('dp', 'head'))
- grad_gate_bias: float32 [8], replicated
- grad_output: float32 [512, 512], P(('dp', 'head'))
- grad_second_gain: float32 [512], P(('dp', 'head'))
- grad_up: float32 [512, 2048], P(('dp', 'head'))
- grad_down: float32 [2048, 512], P(('dp', 'head'))
Inputs may be any that keep to these rules, and one draw needn't show every extreme that they name: `lengths`: in every aligned block of 16 entries (the sentences of one index of dp) one entry equals 1024.
All inputs are finite; a program needn't handle non-finite values.
Results may differ from a plain program's by a relative error of at most 0.012.
Values may be sent and summed in bfloat16 or wider, within the bound.
No kernel may reach another device: no remote copies, remote signals or barrier semaphores. Data moves between devices by JAX's collectives and lax.ppermute only.
A program may use at most 704 MiB of HBM per device.

v0:
```python
import math

import jax
import jax.numpy as jnp
from jax import lax
from jax.sharding import PartitionSpec as P

HEADS = 8
BLOCK = 128


norm_eps = 1e-05
floor_sq = 0.01
highest = lax.Precision.HIGHEST


def matmul(left, right):
    return jnp.dot(left, right, preferred_element_type=jnp.float32)


def matmul_left(left, right):
    return lax.dot_general(
        left, right, (((0,), (0,)), ((), ())), preferred_element_type=jnp.float32
    )


def matmul_right(left, right):
    return lax.dot_general(
        left, right, (((1,), (1,)), ((), ())), preferred_element_type=jnp.float32
    )


def layer_norm(rows_in, gain_row):
    center = rows_in - jnp.mean(rows_in, axis=-1, keepdims=True)
    spread = jnp.mean(center * center, axis=-1, keepdims=True)
    return center * lax.rsqrt(spread + norm_eps) * gain_row


def random_features(inputs, projection):
    angles = jnp.einsum("lhd,hdf->lhf", inputs, projection, precision=highest)
    scale_factor = 1.0 / math.sqrt(projection.shape[2])
    return jnp.concatenate([jnp.sin(angles), jnp.cos(angles)], axis=-1) * scale_factor


def gated_state(queries, key_rows, values, logits, projection, block_len):
    total_len, head_count, head_size = queries.shape
    span_count = total_len // block_len
    phi_query = random_features(queries, projection).reshape(span_count, block_len, head_count, -1)
    phi_key = random_features(key_rows, projection).reshape(span_count, block_len, head_count, -1)
    value_blocks = values.reshape(span_count, block_len, head_count, head_size)
    log_gate = -jax.nn.softplus(-logits).reshape(span_count, block_len, head_count)
    write_rate = jax.nn.sigmoid(-logits).reshape(span_count, block_len, head_count)
    cum_gate = jnp.cumsum(log_gate, axis=1)
    row_ids = jnp.arange(block_len)
    causal = (row_ids[:, None] >= row_ids[None, :])[None, :, :, None]
    gap_log = cum_gate[:, :, None, :] - cum_gate[:, None, :, :]
    decay_mat = jnp.exp(jnp.where(causal, gap_log, -1e30)) * write_rate[:, None, :, :]
    scores = jnp.einsum("cthf,cjhf->ctjh", phi_query, phi_key, precision=highest) * decay_mat
    numer_part = jnp.einsum("ctjh,cjhd->cthd", scores, value_blocks, precision=highest)
    denom_part = jnp.sum(scores, axis=2)
    tail_weight = (jnp.exp(cum_gate[:, -1:, :] - cum_gate) * write_rate)[..., None] * phi_key
    span_state = jnp.einsum("cjhf,cjhd->chfd", tail_weight, value_blocks, precision=highest)
    span_norm = jnp.sum(tail_weight, axis=1)
    span_decay = jnp.exp(cum_gate[:, -1, :])

    def carry_step(carried, inputs):
        state_prev, norm_prev = carried
        add_state, add_norm, keep_rate = inputs
        following = (
            keep_rate[:, None, None] * state_prev + add_state,
            keep_rate[:, None] * norm_prev + add_norm,
        )
        return (following, (state_prev, norm_prev))

    feature_count = phi_key.shape[-1]
    initial = (
        jnp.zeros((head_count, feature_count, head_size), jnp.float32),
        jnp.zeros((head_count, feature_count), jnp.float32),
    )
    ignored, (state_in, norm_in) = lax.scan(
        carry_step, initial, (span_state, span_norm, span_decay)
    )
    lead_decay = jnp.exp(cum_gate)
    numer_part = numer_part + lead_decay[..., None] * jnp.einsum(
        "cthf,chfd->cthd", phi_query, state_in, precision=highest
    )
    denom_part = denom_part + lead_decay * jnp.einsum(
        "cthf,chf->cth", phi_query, norm_in, precision=highest
    )
    attended = numer_part * lax.rsqrt(denom_part * denom_part + floor_sq)[..., None]
    return attended.reshape(total_len, head_count, head_size)


def sentence_heads(query_part, key_part, value_part, logit_part, projection):
    seq_len, width_local = (query_part.shape[1], query_part.shape[2])
    head_local = logit_part.shape[2]
    head_size = width_local // head_local

    def single(query_one, key_one, value_one, logit_one):
        result = gated_state(
            query_one.reshape(seq_len, head_local, head_size),
            key_one.reshape(seq_len, head_local, head_size),
            value_one.reshape(seq_len, head_local, head_size),
            logit_one,
            projection,
            BLOCK,
        )
        return result.reshape(seq_len, width_local)

    return jax.vmap(single)(query_part, key_part, value_part, logit_part)


def body(
    tokens,
    lengths,
    feature_proj,
    first_gain,
    query_weight,
    key_weight,
    value_weight,
    gate_weight,
    gate_bias,
    output_weight,
    second_gain,
    up_weight,
    down_weight,
    cotangent,
):
    params = (
        first_gain,
        query_weight,
        key_weight,
        value_weight,
        gate_weight,
        output_weight,
        second_gain,
        up_weight,
        down_weight,
    )
    gathered = (
        lax.all_gather(params[0], ("dp", "head"), axis=0, tiled=True),
        lax.all_gather(params[1], ("dp", "head"), axis=0, tiled=True),
        lax.all_gather(params[2], ("dp", "head"), axis=0, tiled=True),
        lax.all_gather(params[3], ("dp", "head"), axis=0, tiled=True),
        lax.all_gather(params[4], ("dp", "head"), axis=0, tiled=True),
        lax.all_gather(params[5], ("dp", "head"), axis=0, tiled=True),
        lax.all_gather(params[6], ("dp", "head"), axis=0, tiled=True),
        lax.all_gather(params[7], ("dp", "head"), axis=0, tiled=True),
        lax.all_gather(params[8], ("dp", "head"), axis=0, tiled=True),
    )
    (
        gain_first,
        query_full,
        key_full,
        value_full,
        gate_full,
        output_full,
        gain_second,
        up_full,
        down_full,
    ) = gathered
    slot_count = lengths.shape[0]
    tok_rows = tokens.shape[0]
    piece_len = tok_rows // slot_count
    width = tokens.shape[1]
    head_local = HEADS // lax.axis_size("head")
    head_index = lax.axis_index("head")
    position = head_index * piece_len + jnp.arange(piece_len, dtype=jnp.int32)
    live_mask = (position[None, :] < lengths[:, None]).reshape(tok_rows, 1)
    projection = lax.dynamic_slice_in_dim(feature_proj, head_index * head_local, head_local, 0)
    zero_low = jnp.zeros((), jnp.bfloat16)
    inputs = tokens.astype(jnp.float32)
    normed_one, first_pull = jax.vjp(layer_norm, inputs, gain_first.astype(jnp.float32))
    normed_low = normed_one.astype(jnp.bfloat16)
    queries = matmul(normed_low, query_full).astype(jnp.bfloat16)
    key_rows = matmul(normed_low, key_full).astype(jnp.bfloat16)
    value_rows = matmul(normed_low, value_full).astype(jnp.bfloat16)
    logits = (matmul(normed_low, gate_full) + gate_bias).astype(jnp.bfloat16)
    shaped = (
        queries.reshape(slot_count, piece_len, width),
        key_rows.reshape(slot_count, piece_len, width),
        value_rows.reshape(slot_count, piece_len, width),
        logits.reshape(slot_count, piece_len, HEADS),
    )
    query_part = lax.all_to_all(shaped[0], "head", split_axis=2, concat_axis=1, tiled=True)
    key_part = lax.all_to_all(shaped[1], "head", split_axis=2, concat_axis=1, tiled=True)
    value_part = lax.all_to_all(shaped[2], "head", split_axis=2, concat_axis=1, tiled=True)
    logit_part = lax.all_to_all(shaped[3], "head", split_axis=2, concat_axis=1, tiled=True)
    mixed_heads = sentence_heads(
        query_part.astype(jnp.float32),
        key_part.astype(jnp.float32),
        value_part.astype(jnp.float32),
        logit_part.astype(jnp.float32),
        projection,
    )
    returned = lax.all_to_all(
        mixed_heads.astype(jnp.bfloat16), "head", split_axis=1, concat_axis=2, tiled=True
    )
    moved = returned
    heads_low = jnp.where(live_mask, moved.reshape(tok_rows, width), zero_low)
    middle = inputs + matmul(heads_low, output_full)
    normed_two, second_pull = jax.vjp(layer_norm, middle, gain_second.astype(jnp.float32))
    normed_two_low = normed_two.astype(jnp.bfloat16)
    hidden_pre = matmul(normed_two_low, up_full)
    hidden_act, gelu_pull = jax.vjp(jax.nn.gelu, hidden_pre)
    hidden_low = hidden_act.astype(jnp.bfloat16)
    mixed = (middle + matmul(hidden_low, down_full)).astype(jnp.bfloat16)
    regathered = (
        lax.all_gather(params[0], ("dp", "head"), axis=0, tiled=True),
        lax.all_gather(params[1], ("dp", "head"), axis=0, tiled=True),
        lax.all_gather(params[2], ("dp", "head"), axis=0, tiled=True),
        lax.all_gather(params[3], ("dp", "head"), axis=0, tiled=True),
        lax.all_gather(params[4], ("dp", "head"), axis=0, tiled=True),
        lax.all_gather(params[5], ("dp", "head"), axis=0, tiled=True),
        lax.all_gather(params[6], ("dp", "head"), axis=0, tiled=True),
        lax.all_gather(params[7], ("dp", "head"), axis=0, tiled=True),
        lax.all_gather(params[8], ("dp", "head"), axis=0, tiled=True),
    )
    query_full, key_full, value_full, gate_full, output_full, up_full, down_full = (
        regathered[1],
        regathered[2],
        regathered[3],
        regathered[4],
        regathered[5],
        regathered[7],
        regathered[8],
    )
    upstream = cotangent.astype(jnp.float32)
    grad_down = matmul_left(hidden_low, cotangent)
    grad_hidden = matmul_right(cotangent, down_full)
    grad_pre = gelu_pull(grad_hidden)[0].astype(jnp.bfloat16)
    grad_up = matmul_left(normed_two_low, grad_pre)
    grad_normed_two = matmul_right(grad_pre, up_full)
    grad_middle_part, grad_gain_two = second_pull(grad_normed_two)
    grad_middle = upstream + grad_middle_part
    grad_branch = grad_middle.astype(jnp.bfloat16)
    grad_output = matmul_left(heads_low, grad_branch)
    grad_heads = jnp.where(
        live_mask, matmul_right(grad_branch, output_full).astype(jnp.bfloat16), zero_low
    )
    grad_heads_slots = grad_heads.reshape(slot_count, piece_len, width)

    def local_pull(query_part, key_part, value_part, logit_part, grad_part):

        def run_local(query_in, key_in, value_in, logit_in):
            return sentence_heads(query_in, key_in, value_in, logit_in, projection)

        ignored, pull = jax.vjp(
            run_local,
            query_part.astype(jnp.float32),
            key_part.astype(jnp.float32),
            value_part.astype(jnp.float32),
            logit_part.astype(jnp.float32),
        )
        pulled = pull(grad_part.astype(jnp.float32))
        return (
            pulled[0].astype(jnp.bfloat16),
            pulled[1].astype(jnp.bfloat16),
            pulled[2].astype(jnp.bfloat16),
            pulled[3].astype(jnp.bfloat16),
        )

    grad_part = lax.all_to_all(grad_heads_slots, "head", split_axis=2, concat_axis=1, tiled=True)
    query_part = lax.all_to_all(shaped[0], "head", split_axis=2, concat_axis=1, tiled=True)
    key_part = lax.all_to_all(shaped[1], "head", split_axis=2, concat_axis=1, tiled=True)
    value_part = lax.all_to_all(shaped[2], "head", split_axis=2, concat_axis=1, tiled=True)
    logit_part = lax.all_to_all(shaped[3], "head", split_axis=2, concat_axis=1, tiled=True)
    pulled = local_pull(query_part, key_part, value_part, logit_part, grad_part)
    returned = (
        lax.all_to_all(pulled[0], "head", split_axis=1, concat_axis=2, tiled=True),
        lax.all_to_all(pulled[1], "head", split_axis=1, concat_axis=2, tiled=True),
        lax.all_to_all(pulled[2], "head", split_axis=1, concat_axis=2, tiled=True),
        lax.all_to_all(pulled[3], "head", split_axis=1, concat_axis=2, tiled=True),
    )
    grad_queries = returned[0].reshape(tok_rows, width)
    grad_keys = returned[1].reshape(tok_rows, width)
    grad_values = returned[2].reshape(tok_rows, width)
    grad_logits = returned[3].reshape(tok_rows, HEADS)
    grad_query = matmul_left(normed_low, grad_queries)
    grad_key = matmul_left(normed_low, grad_keys)
    grad_value = matmul_left(normed_low, grad_values)
    grad_gate = matmul_left(normed_low, grad_logits)
    grad_bias_local = jnp.sum(grad_logits.astype(jnp.float32), axis=0)
    grad_normed_one = (
        matmul_right(grad_queries, query_full)
        + matmul_right(grad_keys, key_full)
        + matmul_right(grad_values, value_full)
        + matmul_right(grad_logits, gate_full)
    )
    grad_inputs_part, grad_gain_one = first_pull(grad_normed_one)
    grad_tokens = grad_middle + grad_inputs_part
    reduced = (
        lax.psum_scatter(grad_gain_one, ("dp", "head"), scatter_dimension=0, tiled=True),
        lax.psum_scatter(grad_query, ("dp", "head"), scatter_dimension=0, tiled=True),
        lax.psum_scatter(grad_key, ("dp", "head"), scatter_dimension=0, tiled=True),
        lax.psum_scatter(grad_value, ("dp", "head"), scatter_dimension=0, tiled=True),
        lax.psum_scatter(grad_gate, ("dp", "head"), scatter_dimension=0, tiled=True),
        lax.psum_scatter(grad_output, ("dp", "head"), scatter_dimension=0, tiled=True),
        lax.psum_scatter(grad_gain_two, ("dp", "head"), scatter_dimension=0, tiled=True),
        lax.psum_scatter(grad_up, ("dp", "head"), scatter_dimension=0, tiled=True),
        lax.psum_scatter(grad_down, ("dp", "head"), scatter_dimension=0, tiled=True),
    )
    grad_bias = lax.psum(grad_bias_local, ("dp", "head"))
    return (
        mixed,
        grad_tokens,
        reduced[0],
        reduced[1],
        reduced[2],
        reduced[3],
        reduced[4],
        grad_bias,
        reduced[5],
        reduced[6],
        reduced[7],
        reduced[8],
    )


def solution(mesh):
    placed = (
        P(("dp", "head"), None),
        P("dp"),
        P(),
        P(("dp", "head")),
        P(("dp", "head"), None),
        P(("dp", "head"), None),
        P(("dp", "head"), None),
        P(("dp", "head"), None),
        P(),
        P(("dp", "head"), None),
        P(("dp", "head")),
        P(("dp", "head"), None),
        P(("dp", "head"), None),
        P(("dp", "head"), None),
    )
    return jax.shard_map(
        body,
        mesh=mesh,
        in_specs=placed,
        out_specs=(
            P(("dp", "head"), None),
            P(("dp", "head"), None),
            P(("dp", "head")),
            P(("dp", "head"), None),
            P(("dp", "head"), None),
            P(("dp", "head"), None),
            P(("dp", "head"), None),
            P(),
            P(("dp", "head"), None),
            P(("dp", "head")),
            P(("dp", "head"), None),
            P(("dp", "head"), None),
        ),
        check_vma=False,
    )
```

profile of v0, /device:TPU:0, one launch (start us, length us, event | category | flops | bytes accessed | tf_op | source)
XLA Modules:
  0.0 2909.5 jit_solution(7155732390954621781)
XLA Ops:
  9.0 42.0 %all-reduce.7 = (bf16[512]{0:T(512)(128)(2,1)S(1)}, bf16[512]{0:T(512)(128)(2,1)}) all-reduce(bf16[512]{0:T(512)(128)(2,1)S(1)} %dynamic-update-slice, bf16[512]{0:T(512)(128)(2,1)S(1)} %dynamic-update-slice.1), channel_id=1, replica_groups=mesh['dp'=8,'head'=4] {'dp','head'}, use_global_device_ids=true, to_apply=%add.2 | all-reduce | flops 1024 | bytes 4096
  51.0 40.8 %all-gather = bf16[32,16,8]{1,2,0:T(8,128)(2,1)S(1)} all-gather(bf16[1,16,8]{1,2,0:T(8,128)(2,1)} %bitcast.557), channel_id=1, replica_groups=mesh['dp'=8,'head'=4] {'dp','head'}, dimensions={0}, use_global_device_ids=true | all-gather | bytes 8448 | tf_op jit(solution)/shard_map/all_gather | solution.py:145
  113.9 39.8 %all_gather.37 = bf16[512,512]{1,0:T(8,128)(2,1)S(1)} all-gather(bf16[16,512]{1,0:T(8,128)(2,1)S(1)} %copy-done.100), channel_id=1, replica_groups=mesh['dp'=8,'head'=4] {'dp','head'}, dimensions={0}, use_global_device_ids=true | all-gather | bytes 540672 | tf_op jit(solution)/shard_map/all_gather | solution.py:142
  173.8 79.4 %all_gather.36 = bf16[512,512]{1,0:T(8,128)(2,1)S(1)} all-gather(bf16[16,512]{1,0:T(8,128)(2,1)S(1)} %copy-done.101), channel_id=1, replica_groups=mesh['dp'=8,'head'=4] {'dp','head'}, dimensions={0}, use_global_device_ids=true | all-gather | bytes 540672 | tf_op jit(solution)/shard_map/all_gather | solution.py:143
  273.5 79.4 %all_gather.35 = bf16[512,512]{1,0:T(8,128)(2,1)S(1)} all-gather(bf16[16,512]{1,0:T(8,128)(2,1)S(1)} %copy-done.102), channel_id=1, replica_groups=mesh['dp'=8,'head'=4] {'dp','head'}, dimensions={0}, use_global_device_ids=true | all-gather | bytes 540672 | tf_op jit(solution)/shard_map/all_gather | solution.py:144
  448.5 73.2 %fusion.189 = (f32[2,128,16,1024]{3,1,2,0:T(8,128)}, f32[2,128,16,1024]{3,1,2,0:T(8,128)S(1)}) fusion(bf16[16,1024,2,64]{1,3,2,0:T(8,128)(2,1)} %reshape.314, f32[8,64,128]{2,1,0:T(8,128)S(1)} %copy-done, s32[]{:T(128)S(6)} %select_n.40), kind=kOutput, calls=%fused_computation.282 | convolution fusion | flops 3221225472 | bytes 37814276 | tf_op jit(solution)/shard_map/vmap(lhd,hdf->lhf)/dot_general | solution.py:40
  641.6 73.2 %fusion.188 = (f32[2,128,16,1024]{3,1,2,0:T(8,128)}, f32[2,128,16,1024]{3,1,2,0:T(8,128)S(1)}) fusion(bf16[16,1024,2,64]{1,3,2,0:T(8,128)(2,1)} %reshape.316, f32[8,64,128]{2,1,0:T(8,128)S(1)} %copy-done, s32[]{:T(128)S(6)} %select_n.40), kind=kOutput, calls=%fused_computation.281 | convolution fusion | flops 3221225472 | bytes 37814276 | tf_op jit(solution)/shard_map/vmap(lhd,hdf->lhf)/dot_general | solution.py:40
  775.0 41.1 %fusion.96 = (f32[16,8,128,2]{2,3,1,0:T(2,128)S(1)}, f32[16,8,2,128,128]{4,3,2,1,0:T(8,128)S(1)}) fusion(f32[16,8,128,2]{2,3,1,0:T(2,128)S(1)} %copy-done.57, f32[16,8,128,2]{2,3,1,0:T(2,128)S(1)} %copy-done.31, pred[128,128]{0,1:T(8,128)(4,1)S(1)} %copy-done.78, f32[16,8,128,2,128]{4,2,3,1,0:T(8,128)} %copy.607, f32[16,8,128,2,128]{4,2,3,1,0:T(8,128)} %copy.606, ...), kind=kOutput, calls=%fused_computation.152 | convolution fusion | flops 12939395072 | bytes 84295680 | tf_op jit(solution)/shard_map/vmap(cthf,cjhf->ctjh)/dot_general | solution.py:58
  845.5 89.4 %while.65 = (s32[]{:T(128)}, f32[16,2,256,64]{3,2,1,0:T(8,128)}, f32[16,2,256]{2,1,0:T(2,128)S(1)}, f32[8,16,2,256,64]{4,3,2,1,0:T(8,128)}, f32[8,16,2,256]{3,2,...) while((s32[]{:T(128)}, f32[16,2,256,64]{3,2,1,0:T(8,128)}, ...), condition=%wide.region_12.13_spmd.clone, body=%wide.region_11.12_spmd.clone.sunk | while | flops 2129923 | bytes 31624412 | solution.py:80
  935.0 30.5 %fusion.120 = f32[16,8,2,1,128]{4,3,2,1,0:T(1,128)S(1)} fusion(f32[8,16,2,256,1]{3,2,1,0,4:T(2,128)S(1)} %bitcast.538, f32[16,8,128,2,128]{4,2,3,1,0:T(8,128)} %copy.607, f32[16,8,128,2,128]{4,2,3,1,0:T(8,128)} %copy.606), kind=kOutput, calls=%fused_computation.183 | convolution fusion | flops 117440512 | bytes 33947648 | tf_op jit(solution)/shard_map/jvp(vmap(cthf,chf->cth))/dot_general | solution.py:87
  965.6 82.8 %while.64 = (s32[]{:T(128)}, f32[16,2,256,64]{3,2,1,0:T(8,128)}, f32[16,2,256]{2,1,0:T(2,128)S(1)}, f32[8,16,2,256,64]{4,3,2,0,1:T(8,128)}, f32[8,16,2,256]{3,2,...) while((s32[]{:T(128)}, f32[16,2,256,64]{3,2,1,0:T(8,128)}, ...), condition=%wide.region_5.6_spmd.clone, body=%wide.region_4.5_spmd.clone.sunk | while | flops 2129923 | bytes 31622084 | solution.py:80
  1048.4 30.4 %fusion.122 = f32[16,8,2,1,128]{4,3,2,1,0:T(1,128)S(1)} fusion(f32[8,16,2,256,1]{3,2,1,0,4:T(2,128)S(1)} %bitcast.546, f32[16,8,128,2,128]{4,2,3,1,0:T(8,128)} %copy.607, f32[16,8,128,2,128]{4,2,3,1,0:T(8,128)} %copy.606), kind=kOutput, calls=%fused_computation.185 | convolution fusion | flops 117440512 | bytes 33947648 | tf_op jit(solution)/shard_map/vmap(cthf,chf->cth)/dot_general | solution.py:87
  1079.8 62.8 %fusion.82 = bf16[16,8,128,2,64]{2,4,3,1,0:T(8,128)(2,1)} fusion(f32[16,8,2,64,128]{4,3,2,1,0:T(8,128)} %fusion.97, f32[16,8,128,2]{2,3,1,0:T(2,128)S(1)} %copy.629, f32[16,8,128,2]{2,3,1,0:T(2,128)S(1)} %copy.619, f32[8,16,2,256,64]{4,3,2,0,1:T(8,128)} %get-tuple-element.348, f32[16,8,128,2,128]{4,2,3,1,0:T(8,128)} %copy.607, ...), kind=kOutput, calls=%fused_computation.127 | convolution fusion | flops 6467616768 | bytes 63176704 | tf_op jit(solution)/shard_map/vmap(cthf,chfd->cthd)/dot_general | solution.py:84
  1189.8 78.3 %all_gather.39 = bf16[512,512]{1,0:T(8,128)(2,1)S(1)} all-gather(bf16[16,512]{1,0:T(8,128)(2,1)S(1)} %copy-done.103), channel_id=1, replica_groups=mesh['dp'=8,'head'=4] {'dp','head'}, dimensions={0}, use_global_device_ids=true | all-gather | bytes 540672 | tf_op jit(solution)/shard_map/all_gather | solution.py:146
  1310.9 32.2 %fusion.12 = bf16[4096,2048]{1,0:T(8,128)(2,1)} fusion(f32[4096,2048]{1,0:T(8,128)} %get-tuple-element.854, bf16[4096,512]{1,0:T(8,128)(2,1)} %param.33, bf16[2048,512]{1,0:T(8,128)(2,1)} %all-gather.6.cloned.1.call-done), kind=kOutput, calls=%fused_computation.38 | convolution fusion | flops 8757706752 | bytes 56623104 | tf_op jit(solution)/shard_map/dot_general | solution.py:28
  1391.6 46.7 %all-to-all-done.5 = bf16[16,256,512]{1,0,2:T(8,128)(2,1)} async-done(((bf16[16,256,512]{1,0,2:T(8,128)(2,1)}), bf16[16,256,512]{1,0,2:T(8,128)(2,1)}, u32[]{:S(2)}, u32[]{:S(2)}) %all-to-all-start.5) | async-done | bytes 4194336 | tf_op jit(solution)/shard_map/all_to_all | solution.py:263
  1469.3 69.5 %fusion.79 = (f32[16,8,128,2]{2,3,1,0:T(2,128)}, f32[16,8,128,2]{2,3,1,0:T(2,128)S(1)}, f32[16,8,2,64,128]{4,3,2,1,0:T(8,128)}) fusion(f32[16,8,128,2,64]{2,1,4,3,0:T(8,128)} %reshape.327, f32[16,8,128,2]{2,3,1,0:T(2,128)S(1)} %copy.650, f32[16,8,128,2]{2,3,1,0:T(2,128)S(1)} %copy-done.56, f32[16,8,2,64,128]{4,3,2,1,0:T(8,128)} %fusion.97, ...), kind=kOutput, calls=%fused_computation.123 | convolution fusion | flops 6475939840 | bytes 76021760 | tf_op jit(solution)/shard_map/jvp(vmap(cthf,chfd->cthd))/dot_general | solution.py:84
  1599.1 63.4 %fusion.25 = f32[8,16,2,256,64]{4,3,2,1,0:T(8,128)} fusion(f32[16,8,2,64,128]{4,3,2,1,0:T(8,128)} %get-tuple-element.840, f32[16,8,128,2,128]{4,2,3,1,0:T(8,128)} %copy.607, f32[16,8,128,2,128]{4,2,3,1,0:T(8,128)} %copy.606), kind=kOutput, calls=%fused_computation.58 | convolution fusion | flops 6459228160 | bytes 58720256 | tf_op jit(solution)/shard_map/transpose(jvp(vmap(cthf,chfd->cthd)))/dot_general | solution.py:84
  1673.8 113.5 %while.66 = (s32[]{:T(128)}, f32[16,2,256,64]{3,2,1,0:T(8,128)}, f32[16,2,256]{2,1,0:T(2,128)S(1)}, f32[8,16,2,256,64]{4,3,2,1,0:T(8,128)}, f32[8,16,2,256]{3,2,...) while((s32[]{:T(128)}, f32[16,2,256,64]{3,2,1,0:T(8,128)}, ...), condition=%wide.region_17.18_spmd.clone, body=%wide.region_14.17_spmd.clone.sunk | while | flops 3194852 | bytes 16978248 | solution.py:80
  1811.0 44.2 %fusion.14 = (f32[16,8,128,2]{2,3,1,0:T(2,128)S(1)}, f32[16,8,2,256,128]{3,4,2,1,0:T(8,128)}) fusion(f32[16,8,128,2,128]{4,2,3,1,0:T(8,128)} %copy.601, f32[16,8,128,2,128]{4,2,3,1,0:T(8,128)} %copy.600, bf16[16,8,128,2,64]{2,1,4,3,0:T(8,128)(2,1)S(1)} %copy-done.12, f32[8,16,2,256,64]{4,3,2,1,0:T(8,128)} %get-tuple-element.355, ...), kind=kOutput, calls=%fused_computation.45 | convolution fusion | flops 6484361216 | bytes 88473600 | tf_op jit(solution)/shard_map/transpose(jvp(vmap(cjhf,cjhd->chfd)))/dot_general | solution.py:62
  1948.9 41.1 %fusion.30 = f32[16,8,2,128,256]{4,3,2,1,0:T(8,128)} fusion(f32[16,8,2,128,128]{4,3,2,1,0:T(8,128)} %fusion.74, f32[16,8,2,128]{3,2,1,0:T(2,128)S(1)} %copy.657, f32[16,8,2,128]{3,2,1,0:T(2,128)S(1)} %copy.655, f32[16,8,2,128]{3,2,1,0:T(2,128)S(1)} %copy.653, pred[128,128]{0,1:T(8,128)(4,1)S(1)} %iota_compare_fusion, f32[16,8,128,2,128]{4,2,3,1,0:T(8,128)} %copy.601, ...), kind=kOutput, calls=%fused_computation.64 | convolution fusion | flops 12922650624 | bytes 84295680 | tf_op jit(solution)/shard_map/transpose(jvp(vmap(cthf,cjhf->ctjh)))/dot_general | solution.py:58
  1990.0 51.1 %multiply_bitcast_fusion = f32[16,8,128,2,256]{4,2,3,1,0:T(8,128)} fusion(f32[16,8,2,128,256]{4,3,2,1,0:T(8,128)} %fusion.30, f32[16,8,2,128]{3,2,1,0:T(2,128)S(1)} %copy.647, f32[16,8,2,64,128]{4,3,2,1,0:T(8,128)} %get-tuple-element.840, f32[8,16,2,256,64]{4,3,2,1,0:T(8,128)} %get-tuple-element.1171, f32[8,16,2,256]{3,2,1,0:T(2,128)S(1)} %get-tuple-element.1193), kind=kOutput, calls=%fused_computation.46 | convolution fusion | flops 6476005376 | bytes 92667904 | tf_op jit(solution)/shard_map/transpose(jvp(vmap(cthf,chfd->cthd)))/dot_general | solution.py:84
  2041.1 34.2 %copy.658 = f32[16,8,128,2,256]{2,1,4,0,3:T(8,128)} copy(f32[16,8,128,2,256]{4,2,3,1,0:T(8,128)} %multiply_bitcast_fusion) | data formatting | bytes 67108864 | tf_op jit(solution)/shard_map/transpose(jvp(vmap()))/mul | solution.py:42
  2075.3 35.5 %mul.572 = f32[16,1024,2,256]{1,3,0,2:T(8,128)} reshape(f32[16,8,128,2,256]{2,1,4,0,3:T(8,128)} %copy.658) | data formatting | bytes 67108864 | tf_op jit(solution)/shard_map/transpose(jvp(vmap()))/mul | solution.py:42
  2150.4 54.3 %fusion.13 = f32[16,8,128,2,256]{4,2,3,1,0:T(8,128)} fusion(f32[16,8,2,256,128]{3,4,2,1,0:T(8,128)} %get-tuple-element.857, f32[16,8,128,2]{2,3,1,0:T(2,128)S(1)} %copy.662, f32[16,8,2,128,128]{4,3,2,1,0:T(8,128)} %fusion.74, f32[16,8,2,128]{3,2,1,0:T(2,128)S(1)} %copy.657, f32[16,8,2,128]{3,2,1,0:T(2,128)S(1)} %copy.655, f32[16,8,2,128]{3,2,1,0:T(2,128)S(1)} %copy.653, ...), kind=kOutput, calls=%fused_computation.42 | convolution fusion | flops 12956205056 | bytes 118243328 | tf_op jit(solution)/shard_map/transpose(jvp(vmap(cthf,cjhf->ctjh)))/dot_general | solution.py:58
  2204.6 34.2 %copy.670 = f32[16,8,128,2,256]{2,1,4,0,3:T(8,128)} copy(f32[16,8,128,2,256]{4,2,3,1,0:T(8,128)} %fusion.13) | data formatting | bytes 67108864 | tf_op jit(solution)/shard_map/transpose(jvp(vmap()))/mul | solution.py:42
  2238.9 35.5 %mul.578 = f32[16,1024,2,256]{1,3,0,2:T(8,128)} reshape(f32[16,8,128,2,256]{2,1,4,0,3:T(8,128)} %copy.670) | data formatting | bytes 67108864 | tf_op jit(solution)/shard_map/transpose(jvp(vmap()))/mul | solution.py:42
  2313.8 67.8 %fusion.15 = f32[16,8,2,64,128]{4,3,2,1,0:T(8,128)} fusion(f32[16,8,128,2]{2,3,1,0:T(2,128)S(1)} %copy-done.46, f32[16,8,128,2,128]{4,2,3,1,0:T(8,128)} %copy.601, f32[16,8,128,2,128]{4,2,3,1,0:T(8,128)} %copy.600, f32[8,16,2,256,64]{4,3,2,1,0:T(8,128)} %get-tuple-element.355), kind=kOutput, calls=%fused_computation.48 | convolution fusion | flops 6459228160 | bytes 58851328 | tf_op jit(solution)/shard_map/transpose(jvp(vmap(cjhf,cjhd->chfd)))/dot_general | solution.py:62
  2381.6 39.9 %fusion.101 = bf16[16,8,128,2,64]{2,4,3,1,0:T(8,128)(2,1)} fusion(f32[16,8,2,64,128]{4,3,2,1,0:T(8,128)} %fusion.15, f32[16,8,2,128,128]{4,3,2,1,0:T(8,128)} %copy-done.13, f32[16,8,128,2]{2,3,1,0:T(2,128)S(1)} %copy-done.59, f32[16,8,128,2]{2,3,1,0:T(2,128)S(1)} %copy-done.33, pred[128,128]{0,1:T(8,128)(4,1)S(1)} %copy-done.80, ...), kind=kOutput, calls=%fused_computation.162 | convolution fusion | flops 3244294144 | bytes 38158336 | tf_op jit(solution)/shard_map/transpose(jvp(vmap(ctjh,cjhd->cthd)))/dot_general | solution.py:59
  2578.5 37.3 %all-reduce.6 = (f32[512]{0:T(512)S(1)}, f32[8]{0:T(128)}, f32[512]{0:T(512)S(1)}) all-reduce(f32[512]{0:T(512)S(1)} %get-tuple-element.757, f32[8]{0:T(128)S(1)} %reduce_sum.264, f32[512]{0:T(512)S(1)} %copy-done.109), channel_id=2, replica_groups=mesh['dp'=8,'head'=4] {'dp','head'}, use_global_device_ids=true, to_apply=%region_28.29.clone | all-reduce | flops 1032 | bytes 8256
  2639.6 129.6 %reduce-scatter.12.cloned.1.call-done = f32[16,512]{1,0:T(8,128)} async-done(((f32[512,512]{1,0:T(8,128)}), f32[16,512]{1,0:T(8,128)}) %reduce-scatter.12.cloned.1.call-update) | async-done | bytes 32784 | tf_op jit(solution)/shard_map/reduce_scatter | solution.py:295
  2769.2 133.6 %reduce-scatter.14.cloned.1.call-done = f32[16,512]{1,0:T(8,128)} async-done(((f32[512,512]{1,0:T(8,128)}), f32[16,512]{1,0:T(8,128)}) %reduce-scatter.14.cloned.1.call-update) | async-done | bytes 32784 | tf_op jit(solution)/shard_map/reduce_scatter | solution.py:296
  (699 shorter events, 1271.8 us)
Async XLA Ops:
  7.2 441.3 %copy-start = (f32[8,64,128]{2,1,0:T(8,128)S(1)}, f32[8,64,128]{2,1,0:T(8,128)}, u32[]{:S(2)}) copy-start(f32[8,64,128]{2,1,0:T(8,128)} %param.22) | copy-start | bytes 786436
  110.6 58.3 %all-to-all-start.3 = ((bf16[16,256,8]{1,0,2:T(8,128)(2,1)}), bf16[16,256,8]{1,0,2:T(8,128)(2,1)S(1)}, u32[]{:S(2)}, u32[]{:S(2)}) async-start(bf16[16,256,8]{1,0,2:T(8,128)(2,1)} %copy.609), calls=%async_computation.3 | async-start | bytes 131072 | tf_op jit(solution)/shard_map/all_to_all | solution.py:188
  169.0 99.7 %all-to-all-start.2 = ((bf16[16,256,512]{1,0,2:T(8,128)(2,1)}), bf16[16,256,512]{1,0,2:T(8,128)(2,1)}, u32[]{:S(2)}, u32[]{:S(2)}) async-start(bf16[16,256,512]{1,0,2:T(8,128)(2,1)} %copy.602), calls=%async_computation.2 | async-start | bytes 8388608 | tf_op jit(solution)/shard_map/all_to_all | solution.py:185
  268.6 99.7 %all-to-all-start.1 = ((bf16[16,256,512]{1,0,2:T(8,128)(2,1)}), bf16[16,256,512]{1,0,2:T(8,128)(2,1)}, u32[]{:S(2)}, u32[]{:S(2)}) async-start(bf16[16,256,512]{1,0,2:T(8,128)(2,1)} %copy.596), calls=%async_computation.1 | async-start | bytes 8388608 | tf_op jit(solution)/shard_map/all_to_all | solution.py:186
  368.3 65.5 %all-to-all-start = ((bf16[16,256,512]{1,0,2:T(8,128)(2,1)}), bf16[16,256,512]{1,0,2:T(8,128)(2,1)}, u32[]{:S(2)}, u32[]{:S(2)}) async-start(bf16[16,256,512]{1,0,2:T(8,128)(2,1)} %copy.593), calls=%async_computation | async-start | bytes 8388608 | tf_op jit(solution)/shard_map/all_to_all | solution.py:187
  373.2 911.4 %all-gather.4.cloned.1.call-start = ((), (), s32[]{:S(2)}) async-start(), calls=%async_computation.17 | async-start | bytes 2162688 | tf_op jit(solution)/shard_map/all_gather | solution.py:148
  403.0 193.2 %copy-start.45 = (f32[16,8,128,2]{2,3,1,0:T(2,128)}, f32[16,8,128,2]{2,3,1,0:T(2,128)S(1)}, u32[]{:S(2)}) copy-start(f32[16,8,128,2]{2,3,1,0:T(2,128)S(1)} %copy.622) | copy-start | bytes 393220
  816.1 262.8 %copy-start.60 = (f32[16,8,128,2]{2,3,1,0:T(2,128)}, f32[16,8,128,2]{2,3,1,0:T(2,128)S(1)}, u32[]{:S(2)}) copy-start(f32[16,8,128,2]{2,3,1,0:T(2,128)S(1)} %get-tuple-element.849) | copy-start | bytes 393220
  965.5 113.4 %copy-start.38 = (f32[16,8,2,1,128]{4,3,2,1,0:T(1,128)}, f32[16,8,2,1,128]{4,3,2,1,0:T(1,128)S(1)}, u32[]{:S(2)}) copy-start(f32[16,8,2,1,128]{4,3,2,1,0:T(1,128)S(1)} %fusion.120) | copy-start | bytes 393220
  1177.5 90.7 %all-to-all-start.4 = ((bf16[16,1024,128]{2,0,1:T(8,128)(2,1)}), bf16[16,1024,128]{2,0,1:T(8,128)(2,1)}, u32[]{:S(2)}, u32[]{:S(2)}) async-start(bf16[16,1024,128]{2,0,1:T(8,128)(2,1)} %reshape.344), calls=%async_computation.4 | async-start | bytes 8388608 | tf_op jit(solution)/shard_map/all_to_all | solution.py:196
  1182.5 128.4 %all-gather.6.cloned.1.call-start = ((), (), s32[]{:S(2)}) async-start(), calls=%async_computation.18 | async-start | bytes 2162688 | tf_op jit(solution)/shard_map/all_gather | solution.py:149
  1183.3 176.0 %copy-start.104 = (f32[512]{0:T(512)}, f32[512]{0:T(512)S(1)}, u32[]{:S(2)}) copy-start(f32[512]{0:T(512)S(1)} %convert_element_type.134) | copy-start | bytes 6148
  1183.4 187.3 %copy-start.106 = (pred[4096]{0:T(1024)(128)(4,1)}, pred[4096]{0:T(1024)(128)(4,1)S(1)}, u32[]{:S(2)}) copy-start(pred[4096]{0:T(1024)(128)(4,1)S(1)} %lt.39) | copy-start | bytes 12292
  1280.2 79.1 %copy-start.87 = (f32[4096]{0:T(1024)}, f32[4096]{0:T(1024)S(1)}, u32[]{:S(2)}) copy-start(f32[4096]{0:T(1024)S(1)} %broadcast_multiply_fusion.1) | copy-start | bytes 49156
  1284.5 74.7 %copy-start.96 = (f32[4096]{0:T(1024)}, f32[4096]{0:T(1024)S(1)}, u32[]{:S(2)}) copy-start(f32[4096]{0:T(1024)S(1)} %fusion.165) | copy-start | bytes 49156
  1385.3 53.1 %all-to-all-start.5 = ((bf16[16,256,512]{1,0,2:T(8,128)(2,1)}), bf16[16,256,512]{1,0,2:T(8,128)(2,1)}, u32[]{:S(2)}, u32[]{:S(2)}) async-start(bf16[16,256,512]{1,0,2:T(8,128)(2,1)} %copy.642), calls=%async_computation.5 | async-start | bytes 8388608 | tf_op jit(solution)/shard_map/all_to_all | solution.py:263
  1390.1 1092.7 %reduce-scatter.22.cloned.1.call-start = ((), (), s32[]{:S(2)}) async-start(), calls=%async_computation.25 | async-start | bytes 270336
  1391.6 148.1 %copy-start.34 = (f32[16,8,128,2]{2,3,1,0:T(2,128)}, f32[16,8,128,2]{2,3,1,0:T(2,128)S(1)}, u32[]{:S(2)}) copy-start(f32[16,8,128,2]{2,3,1,0:T(2,128)S(1)} %copy.650) | copy-start | bytes 393220
  1469.3 69.5 %copy-start.39 = (f32[16,8,2,1,128]{4,3,2,1,0:T(1,128)S(1)}, f32[16,8,2,1,128]{4,3,2,1,0:T(1,128)}, u32[]{:S(2)}) copy-start(f32[16,8,2,1,128]{4,3,2,1,0:T(1,128)} %copy-done.38) | copy-start | bytes 393220
  1469.3 70.3 %copy-start.11 = (bf16[16,8,128,2,64]{2,1,4,3,0:T(8,128)(2,1)S(1)}, bf16[16,8,128,2,64]{2,1,4,3,0:T(8,128)(2,1)}, u32[]{:S(2)}) copy-start(bf16[16,8,128,2,64]{2,1,4,3,0:T(8,128)(2,1)} %reshape.312) | copy-start | bytes 12582916
  1673.8 115.4 %copy-start.32 = (f32[16,8,128,2]{2,3,1,0:T(2,128)S(1)}, f32[16,8,128,2]{2,3,1,0:T(2,128)}, u32[]{:S(2)}) copy-start(f32[16,8,128,2]{2,3,1,0:T(2,128)} %copy.612) | copy-start | bytes 393220
  1673.8 115.4 %copy-start.58 = (f32[16,8,128,2]{2,3,1,0:T(2,128)S(1)}, f32[16,8,128,2]{2,3,1,0:T(2,128)}, u32[]{:S(2)}) copy-start(f32[16,8,128,2]{2,3,1,0:T(2,128)} %copy.615) | copy-start | bytes 393220
  1673.8 115.4 %copy-start.79 = (pred[128,128]{0,1:T(8,128)(4,1)S(1)}, pred[128,128]{0,1:T(8,128)(4,1)}, u32[]{:S(2)}) copy-start(pred[128,128]{0,1:T(8,128)(4,1)} %iota_compare_fusion.1) | copy-start | bytes 49156
  1903.3 736.2 %reduce-scatter.16.cloned.1.call-start = ((), (), s32[]{:S(2)}) async-start(), calls=%async_computation.22 | async-start | bytes 1081344 | tf_op jit(solution)/shard_map/reduce_scatter | solution.py:298
  1911.5 728.1 %reduce-scatter.20.cloned.1.call-start = ((), (), s32[]{:S(2)}) async-start(), calls=%async_computation.24 | async-start | bytes 4325376 | tf_op jit(solution)/shard_map/reduce_scatter | solution.py:301
  1926.6 713.0 %reduce-scatter.18.cloned.1.call-start = ((), (), s32[]{:S(2)}) async-start(), calls=%async_computation.23 | async-start | bytes 4325376 | tf_op jit(solution)/shard_map/reduce_scatter | solution.py:300
  2145.1 163.8 %all-to-all-start.6 = ((bf16[16,1024,128]{2,0,1:T(8,128)(2,1)}), bf16[16,1024,128]{2,0,1:T(8,128)(2,1)}, u32[]{:S(2)}, u32[]{:S(2)}) async-start(bf16[16,1024,128]{2,0,1:T(8,128)(2,1)} %copy.660), calls=%async_computation.6 | async-start | bytes 8388608 | tf_op jit(solution)/shard_map/all_to_all | solution.py:270
  2308.9 147.3 %all-to-all-start.7 = ((bf16[16,1024,128]{2,0,1:T(8,128)(2,1)}), bf16[16,1024,128]{2,0,1:T(8,128)(2,1)}, u32[]{:S(2)}, u32[]{:S(2)}) async-start(bf16[16,1024,128]{2,0,1:T(8,128)(2,1)} %copy.672), calls=%async_computation.7 | async-start | bytes 8388608 | tf_op jit(solution)/shard_map/all_to_all | solution.py:271
  2456.1 69.5 %all-to-all-start.8 = ((bf16[16,1024,128]{2,0,1:T(8,128)(2,1)}), bf16[16,1024,128]{2,0,1:T(8,128)(2,1)}, u32[]{:S(2)}, u32[]{:S(2)}) async-start(bf16[16,1024,128]{2,0,1:T(8,128)(2,1)} %reshape.345), calls=%async_computation.8 | async-start | bytes 8388608 | tf_op jit(solution)/shard_map/all_to_all | solution.py:272
  2461.0 178.6 %reduce-scatter.10.cloned.1.call-start = ((), (), s32[]{:S(2)}) async-start(), calls=%async_computation.19 | async-start | bytes 1081344 | tf_op jit(solution)/shard_map/reduce_scatter | solution.py:294
  2502.6 266.5 %reduce-scatter.12.cloned.1.call-start = ((), (), s32[]{:S(2)}) async-start(), calls=%async_computation.20 | async-start | bytes 1081344 | tf_op jit(solution)/shard_map/reduce_scatter | solution.py:295
  2553.7 349.1 %reduce-scatter.14.cloned.1.call-start = ((), (), s32[]{:S(2)}) async-start(), calls=%async_computation.21 | async-start | bytes 1081344 | tf_op jit(solution)/shard_map/reduce_scatter | solution.py:296
  (128 other events, 1884.8 us)
Sparse Core Ops, SparseCore 0:
  376.9 57.0 all-gather.3
  1186.2 57.0 all-gather.5
  1903.5 129.3 reduce-scatter.21
  2035.7 131.0 reduce-scatter.15
  2169.5 137.3 reduce-scatter.19
  2309.6 138.0 reduce-scatter.17
  2502.8 132.6 reduce-scatter.9
  2638.4 130.7 reduce-scatter.11
  2772.0 130.7 reduce-scatter.13
where the time goes:
time: 2930 us; the launch traced here: 2910 us
  matrix products  1080 us (37%)
  local copies, waits for them, and re-layouts  706 us (24%)
  blocking collectives  404 us (14%)
  other arithmetic  345 us (12%)
  waiting for transfers between devices  311 us (11%)
  starting transfers between devices  44 us (2%)
    dot_general x4, matrix products, gated_state(): jnp.einsum('cthf,chfd->cthd', phi_query, state_in, precision=highest)  247 us
    dot_general x4, matrix products, random_features(): angles = jnp.einsum('lhd,hdf->lhf', inputs, projection, precision=highest)  196 us
    mul x4, local copies, waits for them, and re-layouts, random_features(): jnp.concatenate([jnp.sin(angles), jnp.cos(angles)], axis=-1) * scale_factor  139 us
    dot_general x3, matrix products, gated_state(): jnp.einsum('cthf,cjhf->ctjh', phi_query, phi_key, precision=highest)  136 us
    unnamed x245, local copies, waits for them, and re-layouts  135 us
    dot_general x3, matrix products, gated_state(): jnp.einsum('cjhf,cjhd->chfd', tail_weight, value_blocks, precision=highest)  134 us
    reduce_scatter x1, waiting for transfers between devices, body(): lax.psum_scatter(grad_value, ('dp', 'head'), scatter_dimension=0, tiled=T...  134 us
    reduce_scatter x1, waiting for transfers between devices, body(): lax.psum_scatter(grad_key, ('dp', 'head'), scatter_dimension=0, tiled=True)  130 us
  transfers between devices with their start and end apart: 18, of which 3 were waited for; matrix products, arithmetic and copies ran while one was open for 53% of the time, Pallas kernels for 0%

commit v1 on v0

v1 whole, which is shorter than its diff:
```python
import functools
import math

import jax
import jax.numpy as jnp
from jax import lax
from jax.experimental import pallas as pl
from jax.experimental.pallas import tpu as pltpu
from jax.sharding import PartitionSpec as P

HEADS = 8
HD = 64
FEAT = 128
PHI = 2 * FEAT
PAIRS = HEADS // 2
TILE = 128
STATE_ROWS = HEADS * HD + 16

norm_eps = 1e-05
floor_sq = 0.01
f32 = jnp.float32
bf16 = jnp.bfloat16

ROOT_2_PI = math.sqrt(2.0 / math.pi)


def dot(left, right):
    return jnp.dot(left, right, preferred_element_type=f32)


def dot_t(left, right):
    return lax.dot_general(left, right, (((1,), (1,)), ((), ())), preferred_element_type=f32)


def t_dot(left, right):
    return lax.dot_general(left, right, (((0,), (0,)), ((), ())), preferred_element_type=f32)


def sincos_turns(turns):
    r = turns - jnp.round(turns)
    s = r * r
    half_sin = r * (4.4428679 + s * (-7.30744346 + s * (3.59478832 + s * -0.78437455)))
    half_cos = 1.41420413 + s * (-6.9776436 + s * (5.71525082 + s * -1.72837716))
    return half_sin * half_cos, 1.0 - half_sin * half_sin


def exact_sum(mask, values):
    high = values.astype(bf16)
    rest = values - high.astype(f32)
    mid = rest.astype(bf16)
    low = (rest - mid.astype(f32)).astype(bf16)
    return dot(mask, high) + dot(mask, mid) + dot(mask, low)


def iota(shape, axis):
    return lax.broadcasted_iota(jnp.int32, shape, axis)


def tiles_of(rows, step):
    return [slice(r, r + step) for r in range(0, rows, step)]


def pair_masks(rows):
    lane = iota((rows, TILE), 1)
    return lane < HD, lane >= HD


def whole_spec(array):
    shape = array.shape
    return pl.BlockSpec(shape, lambda i, *_: (0,) * len(shape))


def row_spec(block, first):
    rest = (0,) * (len(block) - 1)
    return pl.BlockSpec(block, lambda i, *_: (i + first,) + rest)


ANY_SPEC = pl.BlockSpec(memory_space=pl.ANY)


def staged_call(kernel, name, steps, ins, in_specs, outs, out_specs, kept, after, flops, moved,
                scratch=(), prefetch=()):
    extra = list(kept) + list(after)
    head = len(prefetch) + len(ins)

    def trimmed(*refs):
        kernel(*refs[:head], *refs[head + len(extra):])

    return pl.pallas_call(
        trimmed,
        grid_spec=pltpu.PrefetchScalarGridSpec(
            num_scalar_prefetch=len(prefetch),
            grid=(steps,),
            in_specs=list(in_specs) + [ANY_SPEC] * len(extra),
            out_specs=list(out_specs),
            scratch_shapes=list(scratch),
        ),
        out_shape=list(outs),
        input_output_aliases={head + j: j for j in range(len(kept))},
        compiler_params=pltpu.CompilerParams(vmem_limit_bytes=60 * 2**20),
        cost_estimate=pl.CostEstimate(flops=flops, bytes_accessed=moved, transcendentals=0),
        name=name,
    )(*prefetch, *ins, *extra)


def merged_state(index, odd, arrivals, out_ref):
    near_ref, cross_ref, swap_ref = arrivals

    def both(rows):
        cross = cross_ref[index, rows, :].astype(f32)
        swapped = swap_ref[index, rows, :].astype(f32)
        return jnp.where(odd, swapped, cross), jnp.where(odd, cross, swapped)

    block = slice(HEADS * HD, STATE_ROWS)
    near = near_ref[index, block, :].astype(f32)
    second, first = both(block)
    keep_second = second[8:16]
    keep_near = jnp.where(odd, near[8:16], 1.0)
    for head in range(HEADS):
        rows = slice(head * HD, (head + 1) * HD)
        state, older = both(rows)
        state = state + keep_second[head:head + 1] * older
        out_ref[index, rows, :] = (near_ref[index, rows, :].astype(f32)
                                   + keep_near[head:head + 1] * state).astype(bf16)
    norm = near[0:8] + keep_near * (second[0:8] + keep_second * first[0:8])
    out_ref[index, block, :] = jnp.concatenate([norm, jnp.zeros_like(norm)], axis=0).astype(bf16)


def join_kernel(own_ref, came_ref, out_ref):
    for i in range(own_ref.shape[0]):
        block = slice(HEADS * HD, STATE_ROWS)
        own = own_ref[i, block, :].astype(f32)
        came = came_ref[i, block, :].astype(f32)
        keep = own[8:16]
        for head in range(HEADS):
            rows = slice(head * HD, (head + 1) * HD)
            out_ref[i, rows, :] = (own_ref[i, rows, :].astype(f32)
                                   + keep[head:head + 1] * came_ref[i, rows, :].astype(f32)).astype(bf16)
        out_ref[i, block, :] = jnp.concatenate(
            [own[0:8] + keep * came[0:8], keep * came[8:16]], axis=0).astype(bf16)


def join_states(own, came):
    steps = 2
    spec = row_spec((own.shape[0] // steps,) + own.shape[1:], 0)
    return staged_call(join_kernel, "join", steps, [own, came], [spec, spec],
                       [jax.ShapeDtypeStruct(own.shape, bf16)], [spec], (), (),
                       own.size * 4, own.size * 6)[0]


def write_features(source, proj_ref, out_ref):
    for pair in range(PAIRS):
        part = source[:, pair * TILE:(pair + 1) * TILE]
        angle = dot(jnp.concatenate([part, part], axis=1), proj_ref[pair])
        start = 2 * pair * PHI
        for tile in tiles_of(source.shape[0], 64):
            sine, cosine = sincos_turns(angle[tile])
            sine = sine.astype(bf16)
            cosine = cosine.astype(bf16)
            out_ref[tile, start:start + FEAT] = sine[:, :FEAT]
            out_ref[tile, start + FEAT:start + 2 * FEAT] = cosine[:, :FEAT]
            out_ref[tile, start + 2 * FEAT:start + 3 * FEAT] = sine[:, FEAT:]
            out_ref[tile, start + 3 * FEAT:start + 4 * FEAT] = cosine[:, FEAT:]


def key_kernel(piece, x_ref, gain_ref, w_ref, bias_ref, proj_ref,
               n_ref, pk_ref, v_ref, gc_ref, gr_ref, st_ref):
    total, width = x_ref.shape
    gain = gain_ref[...]
    for tile in tiles_of(total, 128):
        x = x_ref[tile, :].astype(f32)
        center = x - jnp.mean(x, axis=1, keepdims=True)
        spread = jnp.mean(center * center, axis=1, keepdims=True)
        n_ref[tile, :] = (center * lax.rsqrt(spread + norm_eps) * gain).astype(bf16)
    normed = n_ref[...]
    logits = (dot(normed, w_ref[:, 3 * width:]) + bias_ref[...]).astype(bf16).astype(f32)
    soft = jnp.log1p(jnp.exp(-jnp.abs(logits)))
    log_gate = jnp.minimum(logits, 0.0) - soft
    log_write = -jnp.maximum(logits, 0.0) - soft
    keys = dot(normed, w_ref[:, width:2 * width]).astype(bf16)
    values = dot(normed, w_ref[:, 2 * width:3 * width]).astype(bf16)
    v_ref[...] = values
    lower = (iota((piece, piece), 0) >= iota((piece, piece), 1)).astype(bf16)
    lane = iota((piece, TILE), 1)
    count = total // piece
    tails = []
    keeps = []
    for i in range(count):
        rows = slice(i * piece, (i + 1) * piece)
        cum = exact_sum(lower, log_gate[rows])
        delay = cum - log_write[rows] + math.log(FEAT)
        packed = jnp.where(lane < 8, cum, jnp.where(lane < 16, delay, logits[rows]))
        gc_ref[rows, :] = packed
        turned = packed.T
        gr_ref[i] = turned[0:16]
        last = turned[0:8, piece - 1:piece]
        tails.append(jnp.exp(last - turned[8:16]))
        keeps.append(jnp.broadcast_to(jnp.exp(last), (8, PHI)))
    write_features(keys, proj_ref, pk_ref)
    sub = iota((8, PHI), 0)
    for i in range(count):
        rows = slice(i * piece, (i + 1) * piece)
        norm_rows = jnp.zeros((8, PHI), f32)
        tail_low = jnp.concatenate([tails[i], jnp.zeros_like(tails[i])], axis=0).astype(bf16)
        for pair in range(PAIRS):
            turned = values[rows, pair * TILE:(pair + 1) * TILE].astype(f32).T
            for side in range(2):
                head = 2 * pair + side
                scaled = (turned[side * HD:(side + 1) * HD] * tails[i][head:head + 1]).astype(bf16)
                left = jnp.concatenate([scaled, tail_low], axis=0)
                state = dot(left, pk_ref[rows, head * PHI:(head + 1) * PHI])
                st_ref[i, head * HD:(head + 1) * HD, :] = state[0:HD].astype(bf16)
                norm_rows = jnp.where(sub == head, state[HD:HD + 8], norm_rows)
        st_ref[i, HEADS * HD:STATE_ROWS, :] = jnp.concatenate([norm_rows, keeps[i]], axis=0).astype(bf16)


def key_call(x, gain, weights, gate_b, proj, piece, per, sents, first, kept, after):
    total, width = x.shape
    all_sents = total // piece
    tall = lambda cols: row_spec((per * piece, cols), first // per)
    return staged_call(
        functools.partial(key_kernel, piece), "keys", sents // per,
        [x, gain, weights, gate_b, proj],
        [tall(width)] + [whole_spec(a) for a in (gain, weights, gate_b, proj)],
        [
            jax.ShapeDtypeStruct((total, width), bf16),
            jax.ShapeDtypeStruct((total, HEADS * PHI), bf16),
            jax.ShapeDtypeStruct((total, width), bf16),
            jax.ShapeDtypeStruct((total, TILE), f32),
            jax.ShapeDtypeStruct((all_sents, 16, piece), f32),
            jax.ShapeDtypeStruct((sents, STATE_ROWS, PHI), bf16),
        ],
        [tall(width), tall(HEADS * PHI), tall(width), tall(TILE),
         row_spec((per, 16, piece), first // per), row_spec((per, STATE_ROWS, PHI), 0)],
        kept, after, 2 * sents * piece * width * 3 * width * 3, sents * piece * HEADS * PHI * 3)


def query_kernel(n_ref, w_ref, proj_ref, pq_ref):
    width = n_ref.shape[1]
    write_features(dot(n_ref[...], w_ref[:, 0:width]).astype(bf16), proj_ref, pq_ref)


def query_call(n, weights, proj, after):
    total, width = n.shape
    rows = min(512, total)
    return staged_call(
        query_kernel, "queries", total // rows, [n, weights, proj],
        [row_spec((rows, width), 0), whole_spec(weights), whole_spec(proj)],
        [jax.ShapeDtypeStruct((total, HEADS * PHI), bf16)], [row_spec((rows, HEADS * PHI), 0)], (), after,
        total * width * width, total * width)


def staggered(units, stages, stagger):
    if not stagger:
        for unit in units:
            for stage in stages:
                stage(*unit)
        return
    for turn in range(len(units) + len(stages) - 1):
        for place, stage in enumerate(stages):
            if 0 <= turn - place < len(units):
                stage(*units[turn - place])


def pick(side_even, first, second):
    return jnp.where(side_even, first, second)


def state_pair(st_ref, index, pair):
    even = 2 * pair
    top = st_ref[index, even * HD:(even + 1) * HD, :]
    bottom = st_ref[index, (even + 1) * HD:(even + 2) * HD, :]
    base = HEADS * HD
    block = st_ref[index, base:STATE_ROWS, :].astype(f32)
    norm_even = jnp.broadcast_to(block[even:even + 1], (HD, PHI)).astype(bf16)
    norm_odd = jnp.broadcast_to(block[even + 1:even + 2], (HD, PHI)).astype(bf16)
    return top, bottom, norm_even, norm_odd


def middle_kernel(piece, first_sent, stagger, cuts, bound_ref, x_ref, cot_ref, pq_ref, pk_ref, v_ref, gc_ref, gr_ref,
                  near_ref, far_ref, late_ref, gain_ref, w_ref, seg_ref,
                  mixed_ref, gm_ref, heads_ref, n_ref, act_ref, gpre_ref, dn_ref, st_ref, *rest):
    ad_ref, numer_ref, den_ref, mid_ref, hat_ref, low_ref = rest[len(cuts):]
    step = pl.program_id(0)
    total, width = x_ref.shape
    hidden = act_ref.shape[1]
    count = total // piece
    tiles = piece // TILE
    even_lane, odd_lane = pair_masks(piece)
    ones_even = even_lane.astype(bf16)
    ones_odd = odd_lane.astype(bf16)
    diag = iota((TILE, TILE), 0) >= iota((TILE, TILE), 1)
    zero_tile = jnp.zeros((TILE, TILE), bf16)
    units = [(i, pair) for i in range(count) for pair in range(PAIRS)]
    held = {}

    def span(i):
        return slice(i * piece, (i + 1) * piece)

    def start(i, pair):
        rows = span(i)
        scores = []
        for side in range(2):
            head = 2 * pair + side
            feats = slice(head * PHI, (head + 1) * PHI)
            scores.append(dot_t(pq_ref[rows, feats], pk_ref[rows, feats]))
        top, bottom, norm_even, norm_odd = state_pair(st_ref, i, pair)
        blank = jnp.zeros((HD, PHI), bf16)
        carried = jnp.concatenate([
            jnp.concatenate([top, blank], axis=1), jnp.concatenate([blank, bottom], axis=1),
            jnp.concatenate([norm_even, blank], axis=1),
            jnp.concatenate([blank, norm_odd], axis=1)], axis=0)
        outer = dot_t(pq_ref[rows, 2 * pair * PHI:(2 * pair + 2) * PHI], carried)
        held[i, pair] = scores, outer

    def weigh(i, pair):
        scores, outer = held[i, pair]
        lefts = []
        for side in range(2):
            head = 2 * pair + side
            lines = []
            for a in range(tiles):
                lead = gc_ref[i * piece + a * TILE:i * piece + (a + 1) * TILE, head:head + 1]
                line = []
                for b in range(tiles):
                    if b > a:
                        line.append(zero_tile)
                        continue
                    gap = lead - gr_ref[i, 8 + head:9 + head, b * TILE:(b + 1) * TILE]
                    if a == b:
                        gap = jnp.where(diag, gap, -1e30)
                    part = scores[side][a * TILE:(a + 1) * TILE, b * TILE:(b + 1) * TILE]
                    line.append((jnp.exp(gap) * part).astype(bf16))
                lines.append(jnp.concatenate(line, axis=1))
            lefts.append(jnp.concatenate(lines, axis=0))
        held[i, pair] = lefts, outer

    def mix(i, pair):
        lefts, outer = held[i, pair]
        value = v_ref[span(i), pair * TILE:(pair + 1) * TILE]
        right = jnp.concatenate([
            jnp.concatenate([value * ones_even, ones_even], axis=1),
            jnp.concatenate([value * ones_odd, ones_odd], axis=1)], axis=0)
        held[i, pair] = dot(jnp.concatenate(lefts, axis=1), right), outer

    def attend(i, pair):
        inner, outer = held.pop((i, pair))
        cols = slice(pair * TILE, (pair + 1) * TILE)
        bound = bound_ref[first_sent + step * count + i]
        for tile in tiles_of(piece, TILE):
            rows = slice(i * piece + tile.start, i * piece + tile.stop)
            lead = jnp.exp(pick(even_lane[tile], gc_ref[rows, 2 * pair:2 * pair + 1],
                                gc_ref[rows, 2 * pair + 1:2 * pair + 2]))
            numer = inner[tile, :TILE] + lead * outer[tile, :TILE]
            den = inner[tile, TILE:] + lead * outer[tile, TILE:]
            numer_ref[rows, cols] = numer
            den_ref[rows, cols] = den
            attended = numer * lax.rsqrt(den * den + floor_sq)
            live = iota((TILE, TILE), 0) < bound - tile.start
            heads_ref[rows, cols] = jnp.where(live, attended, 0.0).astype(bf16)

    for i in range(count):
        merged_state(i, bound_ref[bound_ref.shape[0] - 1] > 0, (near_ref, far_ref, late_ref), st_ref)
    staggered(units, [start, weigh, mix, attend], stagger)

    proj = dot(heads_ref[...], w_ref[:, hidden:hidden + width])
    gain = gain_ref[...]
    scales = []
    for tile in tiles_of(total, 128):
        middle = x_ref[tile, :].astype(f32) + proj[tile]
        center = middle - jnp.mean(middle, axis=1, keepdims=True)
        spread = jnp.mean(center * center, axis=1, keepdims=True)
        scale = lax.rsqrt(spread + norm_eps)
        xhat = center * scale
        mid_ref[tile, :] = middle
        hat_ref[tile, :] = xhat
        scales.append(scale)
        n_ref[tile, :] = (xhat * gain).astype(bf16)
    normed = n_ref[...]
    cot = cot_ref[...]
    chunks = list(range(hidden // width))

    def chunk_cols(c):
        return (slice(c * width, (c + 1) * width),
                slice(hidden + (c + 1) * width, hidden + (c + 2) * width))

    def raise_up(c):
        cols, down_cols = chunk_cols(c)
        held[c] = dot(normed, w_ref[:, cols]), dot_t(cot, w_ref[:, down_cols])

    def activate(c):
        cols, _ = chunk_cols(c)
        all_pre, all_back = held.pop(c)
        for tile in tiles_of(total, 32):
            pre = all_pre[tile]
            square = pre * pre
            th = jnp.tanh(pre * (ROOT_2_PI + (ROOT_2_PI * 0.044715) * square))
            half = 0.5 + 0.5 * th
            slope = half + (pre * (half - half * half)) * (
                2.0 * ROOT_2_PI + (6.0 * ROOT_2_PI * 0.044715) * square)
            act_ref[tile, cols] = (pre * half).astype(bf16)
            gpre_ref[tile, cols] = (slope * all_back[tile]).astype(bf16)

    def bring_down(c):
        cols, down_cols = chunk_cols(c)
        mixed = dot(act_ref[:, cols], w_ref[:, down_cols])
        grad_n = dot_t(gpre_ref[:, cols], w_ref[:, cols])
        if "sums" in held:
            mixed = held["sums"][0] + mixed
            grad_n = held["sums"][1] + grad_n
        held["sums"] = mixed, grad_n

    staggered([(c,) for c in chunks], [raise_up, activate, bring_down], stagger)
    mixed, grad_n = held.pop("sums")
    for number, tile in enumerate(tiles_of(total, 128)):
        mixed_ref[tile, :] = (mid_ref[tile, :] + mixed[tile]).astype(bf16)
        xhat = hat_ref[tile, :]
        gy = grad_n[tile] * gain
        first = jnp.mean(gy, axis=1, keepdims=True)
        second = jnp.mean(gy * xhat, axis=1, keepdims=True)
        grad_m = cot_ref[tile, :].astype(f32) + scales[number] * (gy - first - xhat * second)
        gm_ref[tile, :] = grad_m
        low_ref[tile, :] = grad_m.astype(bf16)
    grad_h = dot_t(low_ref[...], w_ref[:, hidden:hidden + width])
    sub = iota((8, PHI), 0)

    def divide(i, pair):
        cols = slice(pair * TILE, (pair + 1) * TILE)
        bound = bound_ref[first_sent + step * count + i]
        grads = []
        sums = []
        for tile in tiles_of(piece, TILE):
            rows = slice(i * piece + tile.start, i * piece + tile.stop)
            live = iota((TILE, TILE), 0) < bound - tile.start
            grad = jnp.where(live, grad_h[rows, cols], 0.0).astype(bf16).astype(f32)
            den = den_ref[rows, cols]
            inv = lax.rsqrt(den * den + floor_sq)
            dn = grad * inv
            along = dn * numer_ref[rows, cols]
            high = along.astype(bf16)
            low = (along - high.astype(f32)).astype(bf16)
            dn_ref[rows, 2 * pair * TILE:(2 * pair + 1) * TILE] = dn.astype(bf16)
            grads.append(dn)
            sums.append(jnp.concatenate([high, low], axis=1))
        seg = dot(jnp.concatenate(sums, axis=0), seg_ref[...])
        held[i, pair] = jnp.concatenate(grads, axis=0), seg

    def gather_state(i, pair):
        dn, seg = held.pop((i, pair))
        cols = slice(pair * TILE, (pair + 1) * TILE)
        grads = []
        for tile in tiles_of(piece, TILE):
            rows = slice(i * piece + tile.start, i * piece + tile.stop)
            den = den_ref[rows, cols]
            inv = lax.rsqrt(den * den + floor_sq)
            dd = -(seg[tile] * (den * (inv * inv)))
            dn_ref[rows, (2 * pair + 1) * TILE:(2 * pair + 2) * TILE] = dd.astype(bf16)
            grads.append(dd)
        turned = dn.T
        turned_d = jnp.concatenate(grads, axis=0).T
        lead_rows = jnp.exp(gr_ref[i, 0:8, :])
        if pair == 0:
            held["norm", i] = jnp.zeros((8, PHI), f32)
        for side in range(2):
            head = 2 * pair + side
            lead = lead_rows[head:head + 1]
            left = jnp.concatenate([turned[side * HD:(side + 1) * HD] * lead,
                                    turned_d[side * HD:side * HD + 16] * lead], axis=0)
            state = dot(left.astype(bf16), pq_ref[span(i), head * PHI:(head + 1) * PHI])
            ad_ref[i, head * HD:(head + 1) * HD, :] = state[0:HD].astype(bf16)
            held["norm", i] = jnp.where(sub == head, state[HD:HD + 8], held["norm", i])
        if pair == PAIRS - 1:
            keep = jnp.broadcast_to(lead_rows[:, piece - 1:piece], (8, PHI))
            ad_ref[i, HEADS * HD:STATE_ROWS, :] = jnp.concatenate(
                [held.pop(("norm", i)), keep], axis=0).astype(bf16)

    staggered(units, [divide, gather_state], stagger)
    for out_ref, (low, high) in zip(rest, cuts):
        @pl.when((step >= low // count) & (step < high // count))
        def _(out_ref=out_ref):
            out_ref[...] = ad_ref[...]


def middle_call(bound, x, cot, pq, pk, v, gc, gr, arrivals, gain, weights, seg, piece, per, form, cuts, sents, first,
                kept, after):
    total, width = x.shape
    hidden = (weights.shape[1] - width) // 2
    all_sents = total // piece
    tall = lambda cols: row_spec((per * piece, cols), first // per)
    state = row_spec((per, STATE_ROWS, PHI), 0)
    return staged_call(
        functools.partial(middle_kernel, piece, first, form, cuts), "middle", sents // per,
        [x, cot, pq, pk, v, gc, gr, *arrivals, gain, weights, seg],
        [tall(width), tall(width), tall(HEADS * PHI), tall(HEADS * PHI), tall(width), tall(TILE),
         row_spec((per, 16, piece), first // per), state, state, state]
        + [whole_spec(a) for a in (gain, weights, seg)],
        [
            jax.ShapeDtypeStruct((total, width), bf16),
            jax.ShapeDtypeStruct((total, width), f32),
            jax.ShapeDtypeStruct((total, width), bf16),
            jax.ShapeDtypeStruct((total, width), bf16),
            jax.ShapeDtypeStruct((total, hidden), bf16),
            jax.ShapeDtypeStruct((total, hidden), bf16),
            jax.ShapeDtypeStruct((total, 2 * width), bf16),
            jax.ShapeDtypeStruct((all_sents, STATE_ROWS, PHI), bf16),
            *(jax.ShapeDtypeStruct((high - low, STATE_ROWS, PHI), bf16) for low, high in cuts),
        ],
        [tall(width), tall(width), tall(width), tall(width), tall(hidden), tall(hidden),
         tall(2 * width), row_spec((per, STATE_ROWS, PHI), first // per),
         *(part_spec((per, STATE_ROWS, PHI), low // per, high // per) for low, high in cuts)],
        kept, after, sents * piece * width * TILE, sents * piece * TILE,
        scratch=[pltpu.VMEM((per, STATE_ROWS, PHI), bf16)] + [pltpu.VMEM((per * piece, width), f32)] * 4 + [pltpu.VMEM((per * piece, width), bf16)],
        prefetch=[bound])


def mlp_grad_kernel(n_ref, gpre_ref, act_ref, cot_ref, heads_ref, gm_ref, out_ref, down_ref):
    step = pl.program_id(0)
    width = n_ref.shape[1]
    wide = act_ref.shape[1] // width
    parts = out_ref.shape[0]
    share = width // parts

    @pl.when(step == 0)
    def _():
        down_ref[...] = jnp.zeros_like(down_ref)
        out_ref[...] = jnp.zeros_like(out_ref)

    normed = n_ref[...].T
    cot = cot_ref[...].T
    for c in range(wide):
        cols = slice(c * width, (c + 1) * width)
        lines = slice((wide + c) * share, (wide + c + 1) * share)
        out_ref[:, lines, :] += dot(normed, gpre_ref[:, cols]).reshape(parts, share, width)
        down_ref[:, cols] += dot(cot, act_ref[:, cols])
    out_ref[:, 2 * wide * share:, :] += dot(heads_ref[...].T, gm_ref[...].astype(bf16)).reshape(
        parts, share, width)

    @pl.when(step == pl.num_programs(0) - 1)
    def _():
        for c in range(wide):
            turned = down_ref[:, c * width:(c + 1) * width].T
            out_ref[:, c * share:(c + 1) * share, :] = turned.reshape(parts, share, width)


def mlp_grad_call(parts, n, gpre, act, cot, heads, gm, after):
    total, width = n.shape
    hidden = act.shape[1]
    rows = min(512, total)
    tall = lambda cols: row_spec((rows, cols), 0)
    packed = jax.ShapeDtypeStruct((parts, (hidden + hidden + width) // parts, width), f32)
    return staged_call(
        mlp_grad_kernel, "mlp_grad", total // rows,
        [n, gpre, act, cot, heads, gm],
        [tall(width), tall(hidden), tall(hidden), tall(width), tall(width), tall(width)],
        [packed], [whole_spec(packed)], (), after,
        2 * total * width * (2 * hidden + width), total * (hidden * 4 + width * 10),
        scratch=[pltpu.VMEM((width, hidden), f32)])


def in_grad_kernel(n_ref, d_ref, out_ref):
    @pl.when(pl.program_id(0) == 0)
    def _():
        out_ref[...] = jnp.zeros_like(out_ref)

    normed = n_ref[...].T
    for c in range(d_ref.shape[1] // TILE // 4 + 1):
        cols = slice(c * 4 * TILE, min((c + 1) * 4 * TILE, d_ref.shape[1]))
        out_ref[:, cols] += dot(normed, d_ref[:, cols])


def in_grad_call(n, d, after):
    total, width = n.shape
    rows = min(1024, total)
    out = jax.ShapeDtypeStruct((width, d.shape[1]), f32)
    return staged_call(
        in_grad_kernel, "in_grad", total // rows, [n, d],
        [row_spec((rows, width), 0), row_spec((rows, d.shape[1]), 0)], [out], [whole_spec(out)], (), after,
        2 * total * width * d.shape[1], total * width * 8)


def turn_kernel(piece, cuts, odd_ref, pq_ref, pk_ref, v_ref, dn_ref, gc_ref, gr_ref, st_ref, *rest):
    step = pl.program_id(0)
    back_ref, out_ref, gb_ref, ad_ref = rest[3 * len(cuts):]
    for number, (low, high) in enumerate(cuts):
        @pl.when((step >= low) & (step < high))
        def _(arrivals=rest[3 * number:3 * number + 3]):
            merged_state(0, odd_ref[0] > 0, arrivals, ad_ref)
    width = v_ref.shape[1]
    tiles = piece // TILE
    even_lane, odd_lane = pair_masks(piece)
    masks = (even_lane.astype(bf16), odd_lane.astype(bf16))
    smalls = [jnp.where(mask, 1.0 / HD, 0.0).astype(bf16) for mask in (even_lane, odd_lane)]
    diag = iota((TILE, TILE), 0) <= iota((TILE, TILE), 1)
    zero_tile = jnp.zeros((TILE, TILE), bf16)
    lane = iota((piece, TILE), 1)
    line_lane = iota((1, TILE), 1)
    cum_last = gc_ref[piece - 1:piece, :]
    blank = jnp.zeros((HD, PHI), bf16)
    odd_row = (iota((2 * TILE, TILE), 0) // HD) % 2
    col_sum = jnp.zeros((piece, TILE), f32)
    tail_sum = jnp.zeros((piece, TILE), f32)
    lead_sum = jnp.zeros((piece, TILE), f32)
    last_line = jnp.zeros((1, TILE), f32)
    row_parts = []

    def diagonal(blocks):
        return jnp.concatenate([
            jnp.concatenate([block, blank] if side == 0 else [blank, block], axis=1)
            for block, side in zip(blocks, (0, 1, 0, 1))], axis=0)

    def lane_sums(values, pair):
        high = values.astype(bf16)
        low = (values - high.astype(f32)).astype(bf16)
        chosen = (iota((2 * TILE, TILE), 1) == 2 * pair + odd_row).astype(bf16)
        return dot(jnp.concatenate([high, low], axis=1), chosen)

    for pair in range(PAIRS):
        cols = slice(pair * TILE, (pair + 1) * TILE)
        wide = slice(2 * pair * PHI, (2 * pair + 2) * PHI)
        value = v_ref[:, cols]
        both = dn_ref[:, 2 * pair * TILE:(2 * pair + 2) * TILE]
        states = state_pair(st_ref, 0, pair)
        adjoints = state_pair(ad_ref, 0, pair)
        state = jnp.concatenate(states, axis=0)
        adjoint = jnp.concatenate(adjoints, axis=0)
        tail = jnp.exp(pick(
            even_lane, cum_last[:, 2 * pair:2 * pair + 1] - gc_ref[:, 8 + 2 * pair:9 + 2 * pair],
            cum_last[:, 2 * pair + 1:2 * pair + 2] - gc_ref[:, 9 + 2 * pair:10 + 2 * pair]))
        lead = jnp.exp(pick(even_lane, gc_ref[:, 2 * pair:2 * pair + 1],
                            gc_ref[:, 2 * pair + 1:2 * pair + 2]))
        tail_value = tail * value.astype(f32)
        tail_small = tail * (1.0 / HD)
        far = dot_t(pk_ref[:, wide], diagonal(adjoints))
        tail_sum = tail_sum + lane_sums(tail_value * far[:, :TILE] + tail_small * far[:, TILE:], pair)
        far = tail * far[:, :TILE]
        lead_dn = lead * both[:, :TILE].astype(f32)
        lead_dd = (lead * (1.0 / HD)) * both[:, TILE:].astype(f32)
        outer = dot_t(pq_ref[:, wide], diagonal(states))
        lead_sum = lead_sum + lane_sums(lead_dn * outer[:, :TILE] + lead_dd * outer[:, TILE:], pair)
        tail_both = jnp.concatenate([tail_value.astype(bf16), tail_small.astype(bf16)], axis=1)
        lead_both = jnp.concatenate([lead_dn.astype(bf16), lead_dd.astype(bf16)], axis=1)
        probs = []
        angles_q = []
        angles_k = []
        for side in range(2):
            head = 2 * pair + side
            feats = slice(head * PHI, (head + 1) * PHI)
            phi_q = pq_ref[:, feats]
            phi_k = pk_ref[:, feats]
            mask = jnp.concatenate([masks[side], masks[side]], axis=1)
            value_h = jnp.concatenate([value * masks[side], smalls[side]], axis=1)
            scores = dot_t(phi_k, phi_q)
            dprob = dot_t(value_h, both)
            prob_lines = []
            ds_lines = []
            sums = [None] * tiles
            col_parts = []
            for a in range(tiles):
                delay = gc_ref[a * TILE:(a + 1) * TILE, 8 + head:9 + head]
                prob_line = []
                ds_line = []
                across = None
                for b in range(tiles):
                    if b < a:
                        prob_line.append(zero_tile)
                        ds_line.append(zero_tile)
                        continue
                    gap = gr_ref[0, head:head + 1, b * TILE:(b + 1) * TILE] - delay
                    if a == b:
                        gap = jnp.where(diag, gap, -1e30)
                    decay = jnp.exp(gap)
                    score = scores[a * TILE:(a + 1) * TILE, b * TILE:(b + 1) * TILE]
                    ds = dprob[a * TILE:(a + 1) * TILE, b * TILE:(b + 1) * TILE] * decay
                    energy = ds * score
                    across = energy if across is None else across + energy
                    down = jnp.sum(energy, axis=0, keepdims=True)
                    sums[b] = down if sums[b] is None else sums[b] + down
                    prob_line.append((decay * score).astype(bf16))
                    ds_line.append(ds.astype(bf16))
                col_parts.append(jnp.sum(across, axis=1, keepdims=True))
                prob_lines.append(jnp.concatenate(prob_line, axis=1))
                ds_lines.append(jnp.concatenate(ds_line, axis=1))
            probs.append(jnp.concatenate(prob_lines, axis=0))
            ds = jnp.concatenate(ds_lines, axis=0)
            row_parts.append(jnp.concatenate(sums, axis=1))
            col_sum = jnp.where(lane == head, jnp.concatenate(col_parts, axis=0), col_sum)
            dphi_k = dot(jnp.concatenate([ds, tail_both * mask], axis=1),
                         jnp.concatenate([phi_q, adjoint], axis=0))
            angles_k.append((dphi_k[:, :FEAT] * phi_k[:, FEAT:].astype(f32)
                             - dphi_k[:, FEAT:] * phi_k[:, :FEAT].astype(f32)).astype(bf16))
            dphi_q = t_dot(ds, phi_k) + dot(lead_both * mask, state)
            angles_q.append((dphi_q[:, :FEAT] * phi_q[:, FEAT:].astype(f32)
                             - dphi_q[:, FEAT:] * phi_q[:, :FEAT].astype(f32)).astype(bf16))
            cross = jnp.sum(st_ref[0, head * HD:(head + 1) * HD, :].astype(f32)
                            * ad_ref[0, head * HD:(head + 1) * HD, :].astype(f32),
                            axis=0, keepdims=True)
            cross = cross + (st_ref[0, HEADS * HD:STATE_ROWS, :].astype(f32)[head:head + 1]
                             * ad_ref[0, HEADS * HD:STATE_ROWS, :].astype(f32)[head:head + 1])
            last_line = jnp.where(line_lane == head, jnp.sum(cross, axis=1, keepdims=True), last_line)
        dn = both[:, :TILE]
        near = dot(jnp.concatenate(probs, axis=1),
                   jnp.concatenate([dn * masks[0], dn * masks[1]], axis=0))
        out_ref[:, 2 * width + pair * TILE:2 * width + (pair + 1) * TILE] = (near + far).astype(bf16)
        back = back_ref[pair]
        out_ref[:, cols] = dot(jnp.concatenate(angles_q, axis=1), back).astype(bf16)
        out_ref[:, width + pair * TILE:width + (pair + 1) * TILE] = dot(
            jnp.concatenate(angles_k, axis=1), back).astype(bf16)
    rows_block = jnp.concatenate(row_parts + [jnp.zeros((TILE - HEADS, piece), f32)], axis=0)
    grad_write = col_sum + tail_sum
    grad_cum = rows_block.T + lead_sum - grad_write
    last_line = (last_line * jnp.exp(cum_last) + jnp.sum(tail_sum, axis=0, keepdims=True))
    upper = (iota((piece, piece), 0) <= iota((piece, piece), 1)).astype(bf16)
    grad_gate = exact_sum(upper, grad_cum) + last_line
    logits = pltpu.roll(gc_ref[...], TILE - 16, 1)
    gate = jax.nn.sigmoid(logits)
    grad_logit = jnp.where(lane < HEADS, grad_gate * jax.nn.sigmoid(-logits) - gate * grad_write, 0.0)
    grad_logit = grad_logit.astype(bf16)
    out_ref[:, 3 * width:] = grad_logit

    @pl.when(step == 0)
    def _():
        gb_ref[...] = jnp.zeros_like(gb_ref)

    gb_ref[0:1, :] += jnp.sum(grad_logit.astype(f32), axis=0, keepdims=True)


def part_spec(block, low, high):
    rest = (0,) * (len(block) - 1)
    return pl.BlockSpec(
        block, lambda i, *_: (jnp.minimum(jnp.maximum(i - low, 0), high - low - 1),) + rest)


def turn_call(odd, pq, pk, v, dn, gc, gr, st, arrival_sets, back, piece, first, kept, after):
    total, width = v.shape
    tall = lambda cols: row_spec((piece, cols), first)
    cuts = []
    for arrivals in arrival_sets:
        low = cuts[-1][1] if cuts else 0
        cuts.append((low, low + arrivals[0].shape[0]))
    sents = cuts[-1][1]
    bias = jax.ShapeDtypeStruct((8, TILE), f32)
    return staged_call(
        functools.partial(turn_kernel, piece, cuts), "turn", sents,
        [pq, pk, v, dn, gc, gr, st, *(a for arrivals in arrival_sets for a in arrivals), back],
        [tall(HEADS * PHI), tall(HEADS * PHI), tall(width), tall(2 * width), tall(TILE),
         row_spec((1, 16, piece), first), row_spec((1, STATE_ROWS, PHI), first),
         *(part_spec((1, STATE_ROWS, PHI), *cut) for cut in cuts for _ in range(3)), whole_spec(back)],
        [jax.ShapeDtypeStruct((total, 3 * width + TILE), bf16), bias],
        [tall(3 * width + TILE), whole_spec(bias)],
        kept, after, sents * piece * piece * PHI, sents * piece * TILE,
        scratch=[pltpu.VMEM((1, STATE_ROWS, PHI), bf16)], prefetch=[odd])


def finish_kernel(x_ref, gm_ref, d_ref, gain_ref, w_ref, out_ref):
    grad_n = dot_t(d_ref[...], w_ref[...])
    gain = gain_ref[...]
    for tile in tiles_of(x_ref.shape[0], 128):
        x = x_ref[tile, :].astype(f32)
        center = x - jnp.mean(x, axis=1, keepdims=True)
        spread = jnp.mean(center * center, axis=1, keepdims=True)
        scale = lax.rsqrt(spread + norm_eps)
        xhat = center * scale
        gy = grad_n[tile] * gain
        first = jnp.mean(gy, axis=1, keepdims=True)
        second = jnp.mean(gy * xhat, axis=1, keepdims=True)
        out_ref[tile, :] = gm_ref[tile, :] + scale * (gy - first - xhat * second)


def finish_call(x, gm, d, gain, weights, rows, first, steps, kept, after):
    total, width = x.shape
    tall = lambda cols: row_spec((rows, cols), first)
    return staged_call(
        finish_kernel, "finish", steps, [x, gm, d, gain, weights],
        [tall(width), tall(width), tall(d.shape[1]), whole_spec(gain), whole_spec(weights)],
        [jax.ShapeDtypeStruct((total, width), f32)], [tall(width)], kept, after,
        2 * rows * steps * width * 3 * width, rows * steps * width * 20)


def mesh_bits():
    bits = []
    for axis in ("head", "dp"):
        size = lax.axis_size(axis)
        bit = 1
        while bit < size:
            bits.append((axis, bit))
            bit *= 2
    return bits


def swap(value, axis, bit):
    size = lax.axis_size(axis)
    return lax.ppermute(value, axis, [(i, i ^ bit) for i in range(size)])


def my_bit(axis, bit):
    return (lax.axis_index(axis) // bit) % 2


def tied(value, behind):
    if not behind:
        return value
    return lax.optimization_barrier((value, *behind))[0]


class Track:
    def __init__(self, rounds, count):
        self.rounds = rounds
        self.left = count
        self.behind = None

    def start(self):
        if self.left:
            self.left -= 1
            sent = self.rounds.send(self.behind)
            self.behind = []
            return [sent]
        return []

    def settle(self, behind):
        if self.behind is not None:
            self.behind = self.behind + [behind]

    def result(self):
        while self.left:
            self.start()
        return self.rounds.send(self.behind)


def gather_rounds(local, order):
    bits = mesh_bits()
    count = len(bits)
    held = local.reshape((1,) * count + local.shape)
    for place in order:
        axis, bit = bits[place]
        sent = held
        other = swap(sent, axis, bit)
        behind = yield sent
        other = tied(other, behind)
        dim = count - 1 - place
        held = jnp.where(my_bit(axis, bit) == 0, jnp.concatenate([held, other], axis=dim),
                         jnp.concatenate([other, held], axis=dim))
    while True:
        yield held.reshape((-1,) + local.shape[1:])


def two_parts(value):
    high = lax.reduce_precision(value, 8, 7)
    return high, lax.reduce_precision(value - high, 8, 7)


def scatter_rounds(total, everywhere, order):
    bits = mesh_bits()
    count = len(bits)
    lanes = everywhere.shape[1]
    wide = total.shape[2]
    held = total.reshape((2,) * count + total.shape[1:])
    for place in order:
        axis, bit = bits[place]
        mine = my_bit(axis, bit)
        dim = count - 1 - place
        send = lax.dynamic_slice_in_dim(held, 1 - mine, 1, dim)
        keep = lax.dynamic_slice_in_dim(held, mine, 1, dim)
        high, low = two_parts(everywhere)
        line = jnp.concatenate([high, low, jnp.zeros((1, wide - 2 * lanes), f32)], axis=1)
        line = jnp.concatenate([line, jnp.zeros((15, wide), f32)], axis=0)
        send = jnp.concatenate([send.reshape(-1, wide), line], axis=0).astype(bf16)
        other = swap(send, axis, bit)
        behind = yield send
        other = tied(other, behind).astype(f32)
        held = keep + other[:-16].reshape(keep.shape)
        everywhere = (high + low) + (other[-16:-15, :lanes] + other[-16:-15, lanes:2 * lanes])
    while True:
        yield held.reshape(total.shape[1:]), everywhere


def carry_rounds(local, reverse):
    size = lax.axis_size("head")
    chips = size // 2

    def hop(value, pairs):
        if reverse:
            pairs = [(size - 1 - a, size - 1 - b) for a, b in pairs]
        return lax.ppermute(value, "head", pairs)

    if chips == 2:
        near = hop(local, [(0, 1), (2, 3)])
        cross = hop(local, [(1, 2), (0, 3)])
        behind = yield local
        near, cross = tied((near, cross), behind)
        swapped = hop(cross, [(2, 3), (3, 2)])
        behind = yield cross
        swapped = tied(swapped, behind)
        while True:
            yield [near, cross, swapped]
    near = hop(local, [(2 * c, 2 * c + 1) for c in range(chips)])
    behind = yield local
    ends = join_states(local, tied(near, behind))
    far = None
    late = None
    for c in range(chips - 1):
        come = hop(ends, [(2 * c + 1, 2 * c + 2)])
        behind = yield ends
        come = tied(come, behind)
        relay = hop(come, [(2 * c + 2, 2 * c + 3)])
        far = come if far is None else far + come
        late = relay if late is None else late + relay
        behind = yield come
        relay = tied(relay, behind)
        if c < chips - 2:
            ends = join_states(local, join_states(near, late))
    while True:
        yield [near, far, late]


def feature_tables(projection):
    turns = projection * (1.0 / (2.0 * math.pi))
    high = lax.reduce_precision(turns, 8, 7)
    low = turns - high

    def blocks(part):
        paired = part.reshape(PAIRS, 2, HD, FEAT)
        blank = jnp.zeros_like(paired[:, 0])
        return jnp.concatenate([
            jnp.concatenate([paired[:, 0], blank], axis=2),
            jnp.concatenate([blank, paired[:, 1]], axis=2)], axis=1)

    forward = jnp.concatenate([blocks(high), blocks(low)], axis=1).astype(bf16)
    backward = blocks(projection).transpose(0, 2, 1).astype(bf16)
    return forward, backward


def body(tokens, lengths, feature_proj, first_gain, query_weight, key_weight, value_weight, gate_weight,
         gate_bias, output_weight, second_gain, up_weight, down_weight, cotangent):
    slots = lengths.shape[0]
    total, width = tokens.shape
    piece = total // slots
    head_index = lax.axis_index("head")
    rows_local = query_weight.shape[0]
    devices = lax.axis_size("dp") * lax.axis_size("head")
    hidden = up_weight.shape[1]
    gains = jnp.stack([first_gain, second_gain], axis=1)
    gate_lanes = jnp.concatenate(
        [gate_weight, gate_weight, gate_weight, gains,
         jnp.zeros((rows_local, TILE - 3 * HEADS - 2), bf16)], axis=1)
    packed = jnp.concatenate([query_weight, key_weight, value_weight, gate_lanes], axis=1)
    count = len(mesh_bits())
    place_order = list(reversed(range(count)))
    first_gather = Track(gather_rounds(packed, place_order), count)
    first_gather.start()
    begun = first_gather.start()
    wide = hidden // width
    up_mixed = tied(up_weight, begun).reshape(rows_local, devices, wide, rows_local).transpose(0, 2, 1, 3)
    down_mixed = tied(down_weight, begun).reshape(wide, rows_local, width).transpose(1, 0, 2)
    middle_weights = lax.all_gather(
        jnp.concatenate([up_mixed.reshape(rows_local, hidden), tied(output_weight, begun),
                         down_mixed.reshape(rows_local, hidden)], axis=1),
        ("dp", "head"), axis=0, tiled=True)
    first_full = first_gather.result()
    gain_lanes = first_full[:, 3 * width + 3 * HEADS:3 * width + 3 * HEADS + 2].astype(f32)
    gain_one = gain_lanes[:, 0][None, :]
    gain_two = gain_lanes[:, 1][None, :]
    gate_b = jnp.concatenate([gate_bias] * 3 + [jnp.zeros((TILE - 3 * HEADS,), f32)])[None, :]
    proj, back = feature_tables(feature_proj)
    lane = jnp.arange(TILE)
    seg = (lane[:, None] // HD == lane[None, :] // HD).astype(bf16)
    seg = jnp.concatenate([seg, seg], axis=0)

    lead_size = slots * 7 // 16
    sizes = [lead_size, slots - lead_size]
    firsts = [0, lead_size]
    chunks = len(sizes)
    chips = lax.axis_size("head") // 2
    hops = 2 if chips == 2 else 2 * chips - 1

    def beside(tracks, call, through=()):
        sent = []
        for track in tracks:
            sent += track.start()
        out = call(sent)
        for track in (*tracks, *through):
            track.settle(out[-1])
        return out

    states = []
    kept = ()
    for k in range(chunks):
        *kept, local = beside(states[k - 1:k] if k else (), lambda after: key_call(
            tokens, gain_one, first_full, gate_b, proj, piece, 1, sizes[k], firsts[k], kept,
            after + ([] if k else [back, seg])), states[:max(k - 1, 0)])
        states.append(Track(carry_rounds(local, False), hops))
    normed, pk, v, gc, gr = kept
    (pq,) = beside(states[-1:], lambda after: query_call(normed, first_full, proj, after), states[:-1])

    bound = jnp.concatenate([lengths - head_index * piece, (head_index % 2)[None]])
    odd_back = (1 - head_index % 2)[None]
    adjoints = []
    kept = ()
    parts = [[(0, sizes[0])], [(0, slots // 4), (slots // 4, sizes[1])]]
    for k in range(chunks):
        arrivals = states[k].result()
        out = beside(adjoints, lambda after: middle_call(
            bound, tokens, cotangent, pq, pk, v, gc, gr, arrivals, gain_two, middle_weights, seg, piece, 1,
            True, parts[k], sizes[k], firsts[k], kept, after), states[k + 1:])
        kept = out[:8]
        adjoints += [Track(carry_rounds(local, True), hops) for local in out[8:]]
    mixed, gm, heads_low, n_two, act, gpre, dn, state_in = kept
    (mlp_grad,) = beside(adjoints[:2], lambda after: mlp_grad_call(
        devices, n_two, gpre, act, cotangent, heads_low, gm, after))
    arrivals = adjoints[0].result()
    begun = adjoints[1].start()
    mlp_part = lax.psum_scatter(tied(mlp_grad, arrivals[-1:] + begun),
                                ("dp", "head"), scatter_dimension=0, tiled=False)
    dqkv, bias_part = beside(adjoints[2:], lambda after: turn_call(
        odd_back, pq, pk, v, dn, gc, gr, state_in, [arrivals], back, piece, 0, (), after + begun),
        adjoints[1:2])
    late_arrivals = [adjoints[1].result(), adjoints[2].result()]
    dqkv, grad_bias = turn_call(
        odd_back, pq, pk, v, dn, gc, gr, state_in, late_arrivals, back, piece, sizes[0], [dqkv], [])
    grad_bias = grad_bias + bias_part
    (in_grad,) = in_grad_call(normed, dqkv, ())
    in_sum = Track(scatter_rounds(in_grad.reshape((devices, -1) + in_grad.shape[1:]), grad_bias[0:1],
                                  list(range(count))), count)
    kept = ()
    blocks = 8 if total % 4096 == 0 else 4
    cuts = [0, (3 * blocks + 4) // 8, (6 * blocks + 4) // 8, blocks]
    for k in range(3):
        kept = beside([in_sum], lambda after: finish_call(
            tokens, gm, dqkv, gain_one, first_full, total // blocks, cuts[k], cuts[k + 1] - cuts[k], kept,
            after + ([mlp_part] if k == 2 else [])))
    grad_tokens = kept[0]
    last, grad_bias = in_sum.result()
    grad_bias = grad_bias[0, :HEADS]
    split = wide * rows_local
    grad_down = mlp_part[:split]
    grad_up = mlp_part[split:2 * split].reshape(wide, rows_local, devices, rows_local).transpose(
        1, 2, 0, 3).reshape(rows_local, hidden)
    grad_output = mlp_part[2 * split:]
    grad_gate = last[:, 3 * width:3 * width + HEADS]
    mine = jnp.concatenate([query_weight, key_weight, value_weight, gate_weight], axis=1).astype(f32)
    grad_first_gain = jnp.sum(mine * last[:, :3 * width + HEADS], axis=1) / first_gain.astype(f32)
    grad_second_gain = jnp.sum(up_weight.astype(f32) * grad_up, axis=1) / second_gain.astype(f32)
    return (
        mixed,
        grad_tokens,
        grad_first_gain,
        last[:, :width],
        last[:, width:2 * width],
        last[:, 2 * width:3 * width],
        grad_gate,
        grad_bias,
        grad_output,
        grad_second_gain,
        grad_up,
        grad_down,
    )


def solution(mesh):
    split = P(("dp", "head"), None)
    line = P(("dp", "head"))
    return jax.shard_map(
        body,
        mesh=mesh,
        in_specs=(split, P("dp"), P(), line, split, split, split, split, P(), split, line, split, split,
                  split),
        out_specs=(split, split, line, split, split, split, split, P(), split, line, split, split),
        check_vma=False,
    )
```

time: 2930 us -> 451 us (0.15)
  matrix products: 1080 us -> 0 us
  local copies, waits for them, and re-layouts: 706 us -> 19.5 us
  blocking collectives: 404 us -> 0 us
  other arithmetic: 345 us -> 7.99 us
  Pallas kernels: 0 us -> 315 us
  waiting for transfers between devices: 311 us -> 33.7 us
    dot_general x40 -> x0, matrix products: 1080 us -> none  [the longest x4 247 us: gated_state(): jnp.einsum('cthf,chfd->cthd', phi_query, state_in, precision=highest)]
    all_gather x5 -> x0, blocking collectives: 318 us -> none  [the longest x1 79.4 us: body(): lax.all_gather(params[2], ('dp', 'head'), axis=0, tiled=True)]
    pallas_call x0 -> x12, Pallas kernels: none -> 315 us  [staged_call(): pl.pallas_call(trimmed, grid_spec=pltpu.PrefetchScalarGridSpec(num_scalar...]
    reduce_scatter x6 -> x1, waiting for transfers between devices: 263 us -> 0.01 us  [body(): lax.psum_scatter(tied(mlp_grad, arrivals[-1:] + begun), ('dp', 'head'), s...]
    mul x72 -> x0, local copies, waits for them, and re-layouts: 153 us -> none  [the longest x4 139 us: random_features(): jnp.concatenate([jnp.sin(angles), jnp.cos(angles)], axis=-1) * scale_factor]
    unnamed x245 -> x59, local copies, waits for them, and re-layouts: 135 us -> 7.56 us
    reduce_sum x25 -> x2, other arithmetic: 123 us -> 0.27 us  [the longest x1 0.14 us: body(): jnp.sum(up_weight.astype(f32) * grad_up, axis=1) / second_gain.astype(f32)]
    convert_element_type x11 -> x0, local copies, waits for them, and re-layouts: 112 us -> none  [the longest x2 34.9 us: body(): mixed_heads.astype(jnp.bfloat16)]
  transfers between devices with their start and end apart: 18 -> 27, of which waited for: 3 -> 10; matrix products, arithmetic and copies ran while one was open for 53% -> 3% of each run, Pallas kernels for 0% -> 71%
where the time goes in v1:
time: 451 us; the launch traced here: 444 us
  Pallas kernels  315 us (70%)
  starting transfers between devices  52.5 us (12%)
  waiting for transfers between devices  33.7 us (7%)
  local copies, waits for them, and re-layouts  19.5 us (4%)
  between operations  15.5 us (3%)
  other arithmetic  7.99 us (2%)
    pallas_call x12, Pallas kernels, staged_call(): pl.pallas_call(trimmed, grid_spec=pltpu.PrefetchScalarGridSpec(num_scalar...  315 us
    ppermute x15, starting transfers between devices, hop(): return lax.ppermute(value, 'head', pairs)  37.1 us
    ppermute x10, waiting for transfers between devices, swap(): return lax.ppermute(value, axis, [(i, i ^ bit) for i in range(size)])  24.5 us
    ppermute x10, starting transfers between devices, swap(): return lax.ppermute(value, axis, [(i, i ^ bit) for i in range(size)])  15.3 us
    ppermute x15, waiting for transfers between devices, hop(): return lax.ppermute(value, 'head', pairs)  9.14 us
  transfers between devices with their start and end apart: 27, of which 10 were waited for; matrix products, arithmetic and copies ran while one was open for 3% of the time, Pallas kernels for 71%

profile of v1, /device:TPU:0, one launch (start us, length us, event | category | flops | bytes accessed | tf_op | source)
XLA Modules:
  0.0 443.8 jit_solution(9677944094883778082)
XLA Ops:
  10.4 4.1 collective-permute-start
  14.5 2.7 collective-permute-done
  21.8 3.3 collective-permute-done.1
  27.0 4.1 collective-permute-done.2
  33.0 7.1 %collective-permute-done.3 = bf16[2,2,2,1,1,16,1664]{6,5,4,3,2,1,0:T(8,128)(2,1)S(1)} collective-permute-done((bf16[2,2,2,1,1,16,1664]{6,5,4,3,2,1,0:T(8,128)(2,1)S(1)}, bf16[2,2,2,1,1,16,1664]{6,5,4,3,2,1,0:T(8,128)(2,1)S(1)}, u32[]{:S(2)}, u32[]{:S(2)}) %collective-permute-start.3) | collective-permute-done | bytes 426016 | tf_op jit(solution)/shard_map/ppermute | solution.py:792
  45.1 15.8 %keys.2 = (bf16[4096,512]{1,0:T(8,128)(2,1)}, bf16[4096,2048]{1,0:T(8,128)(2,1)}, bf16[4096,512]{1,0:T(8,128)(2,1)}, f32[4096,128]{1,0:T(8,128)}, f32[16,16,256]{2,1,0:T(8,128)}, /*index=5*/bf16[7,528,256]{2,1,0:T(8,128)(2,1)}) custom-call(bf16[4096,512]{1,0:T(8,128)(2,1)} %refs_0_.9, f32[1,512]{1,0:T(1,128)} %bitcast.129, bf16[512,1664]{1,0:T(8,128)(2,1)} %bitcast.94, ...), custom_call_target="tpu_custom_call" | custom-call | flops 8455716864 | bytes 11010048 | tf_op jit(solution)/shard_map/keys/pallas_call | solution.py:89
  60.9 3.7 collective-permute-start.7
  64.6 2.5 collective-permute-start.8
  67.1 19.8 %keys.3 = (bf16[4096,512]{1,0:T(8,128)(2,1)}, bf16[4096,2048]{1,0:T(8,128)(2,1)}, bf16[4096,512]{1,0:T(8,128)(2,1)}, f32[4096,128]{1,0:T(8,128)}, f32[16,16,256]{2,1,0:T(8,128)}, /*index=5*/bf16[9,528,256]{2,1,0:T(8,128)(2,1)}) custom-call(bf16[4096,512]{1,0:T(8,128)(2,1)} %refs_0_.9, ...), custom_call_target="tpu_custom_call", output_to_operand_aliasing={{0}: (5, {}), {1}: (6, {}), {2}: (7, {}), {3}: (8, {}), {4}... | custom-call | flops 10871635968 | bytes 14155776 | tf_op jit(solution)/shard_map/keys/pallas_call | solution.py:89
  86.9 4.3 collective-permute-start.5
  91.2 2.7 collective-permute-start.6
  93.9 18.2 %queries.1.refs_3_.refs_1_ = bf16[4096,2048]{1,0:T(8,128)(2,1)} custom-call(bf16[4096,512]{1,0:T(8,128)(2,1)} %get-tuple-element.72.refs_0_, bf16[512,1664]{1,0:T(8,128)(2,1)} %bitcast.96, bf16[4,256,256]{2,1,0:T(8,128)(2,1)} %fusion.7.refs_4_.refs_2_, bf16[9,528,256]{2,1,0:T(8,128)(2,1)} %get-tuple-element.73.refs_3_), custom_call_target="tpu_custom_call" | custom-call | flops 1073741824 | bytes 2097152 | tf_op jit(solution)/shard_map/queries/pallas_call | solution.py:89
  112.1 2.3 collective-permute-done.8.refs_9_
  114.4 2.0 collective-permute-start.9
  117.1 45.0 %middle.2 = (bf16[4096,512]{1,0:T(8,128)(2,1)}, f32[4096,512]{1,0:T(8,128)}, bf16[4096,512]{1,0:T(8,128)(2,1)}, bf16[4096,512]{1,0:T(8,128)(2,1)}, bf16[4096,204...) custom-call(s32[17]{0:T(128)} %pad_add_fusion.refs_0_, ...), custom_call_target="tpu_custom_call" | custom-call | flops 117440512 | bytes 229376 | tf_op jit(solution)/shard_map/middle/pallas_call | solution.py:89
  162.1 4.4 collective-permute-done.6.refs_9_
  166.5 2.1 collective-permute-start.10
  171.2 56.7 %middle.3 = (bf16[4096,512]{1,0:T(8,128)(2,1)}, f32[4096,512]{1,0:T(8,128)}, bf16[4096,512]{1,0:T(8,128)(2,1)}, bf16[4096,512]{1,0:T(8,128)(2,1)}, bf16[4096,204...) custom-call(s32[17]{0:T(128)} %pad_add_fusion.refs_0_, ...), custom_call_target="tpu_custom_call", output_to_operand_aliasing={{0}: (14, {}), {1}: (15, {}), {2}: (16, {}), {3}: (17, {}),... | custom-call | flops 150994944 | bytes 294912 | tf_op jit(solution)/shard_map/middle/pallas_call | solution.py:89
  228.0 4.3 collective-permute-start.16
  235.0 30.8 %mlp_grad.1 = f32[32,144,512]{2,1,0:T(8,128)} custom-call(bf16[4096,512]{1,0:T(8,128)(2,1)} %get-tuple-element.99.refs_0_, bf16[4096,2048]{1,0:T(8,128)(2,1)} %get-tuple-element.100.refs_1_, bf16[4096,2048]{1,0:T(8,128)(2,1)} %get-tuple-element.101.refs_2_, bf16[4096,512]{1,0:T(8,128)(2,1)} %refs_3_.1, bf16[4096,512]{1,0:T(8,128)(2,1)} %get-tuple-element.102.refs_4_, ...), custom_call_target="tpu_custom_call" | custom-call | flops 19327352832 | bytes 54525952 | tf_op jit(solution)/shard_map/mlp_grad/pallas_call | solution.py:89
  270.1 40.0 %turn.2 = (bf16[4096,1664]{1,0:T(8,128)(2,1)}, f32[8,128]{1,0:T(8,128)}) custom-call(s32[1]{0:T(128)} %bitcast.32.refs_0_, bf16[4096,2048]{1,0:T(8,128)(2,1)} %queries.1.refs_3_.refs_1_, bf16[4096,2048]{1,0:T(8,128)(2,1)} %get-tuple-element.74.refs_4_.refs_2_, bf16[4096,512]{1,0:T(8,128)(2,1)} %get-tuple-element.75.refs_5_.refs_3_, ...), custom_call_target="tpu_custom_call" | custom-call | flops 117440512 | bytes 229376 | tf_op jit(solution)/shard_map/turn/pallas_call | solution.py:89
  310.1 5.3 %collective-permute-start.19 = (bf16[5,528,256]{2,1,0:T(8,128)(2,1)S(1)}, bf16[5,528,256]{2,1,0:T(8,128)(2,1)}, u32[]{:S(2)}, u32[]{:S(2)}) collective-permute-start(bf16[5,528,256]{2,1,0:T(8,128)(2,1)S(1)} %collective-permute-done.18.refs_12_), channel_id=1, source_target_pairs={{1,0},{0,1},{5,4},{4,5},{9,8},{8,9},{13,12},{12,13},{17,16},{16,17... | collective-permute-start | bytes 4055048 | tf_op jit(solution)/shard_map/ppermute | solution.py:883
  315.5 2.2 collective-permute-start.15
  317.7 2.4 collective-permute-done.15.refs_10_
  321.1 50.6 %turn.3 = (bf16[4096,1664]{1,0:T(8,128)(2,1)}, f32[8,128]{1,0:T(8,128)}) custom-call(s32[1]{0:T(128)} %bitcast.32.refs_0_, bf16[4096,2048]{1,0:T(8,128)(2,1)} %queries.1.refs_3_.refs_1_, bf16[4096,2048]{1,0:T(8,128)(2,1)} %get-tuple-element.74.refs_4_.refs_2_, bf16[4096,512]{1,0:T(8,128)(2,1)} %get-tuple-element.75.refs_5_.refs_3_, ...), custom_call_target="tpu_custom_call", output_to_operand_aliasing={{0}: (15, {})} | custom-call | flops 150994944 | bytes 294912 | tf_op jit(solution)/shard_map/turn/pallas_call | solution.py:89
  372.4 13.0 %in_grad.1 = f32[512,1664]{1,0:T(8,128)} custom-call(bf16[4096,512]{1,0:T(8,128)(2,1)} %get-tuple-element.72.refs_0_, bf16[4096,1664]{1,0:T(8,128)(2,1)} %get-tuple-element.114.refs_1_.refs_2_), custom_call_target="tpu_custom_call" | custom-call | flops 6979321856 | bytes 16777216 | tf_op jit(solution)/shard_map/in_grad/pallas_call | solution.py:89
  388.0 8.9 %finish.3.refs_5_ = f32[4096,512]{1,0:T(8,128)} custom-call(bf16[4096,512]{1,0:T(8,128)(2,1)} %refs_0_.9, f32[4096,512]{1,0:T(8,128)} %get-tuple-element.95.refs_5_.refs_1_, bf16[4096,1664]{1,0:T(8,128)(2,1)} %get-tuple-element.114.refs_1_.refs_2_, f32[1,512]{1,0:T(1,128)} %bitcast.131, bf16[512,1664]{1,0:T(8,128)(2,1)} %bitcast.97, bf16[272,1664]{1,0:T(8,128)(2,1)} %copy-done.3), custom_call_target="tpu_custom_call" | custom-call | flops 2415919104 | bytes 15728640 | tf_op jit(solution)/shard_map/finish/pallas_call | solution.py:89
  400.0 9.0 %finish.4.refs_5_ = f32[4096,512]{1,0:T(8,128)} custom-call(bf16[4096,512]{1,0:T(8,128)(2,1)} %refs_0_.9, f32[4096,512]{1,0:T(8,128)} %get-tuple-element.95.refs_5_.refs_1_, bf16[4096,1664]{1,0:T(8,128)(2,1)} %get-tuple-element.114.refs_1_.refs_2_, f32[1,512]{1,0:T(1,128)} %bitcast.132, bf16[512,1664]{1,0:T(8,128)(2,1)} %bitcast.98, ...), custom_call_target="tpu_custom_call", output_to_operand_aliasing={{}: (5, {})} | custom-call | flops 2415919104 | bytes 15728640 | tf_op jit(solution)/shard_map/finish/pallas_call | solution.py:89
  408.9 3.4 collective-permute-done.21
  414.4 6.9 %finish.5 = f32[4096,512]{1,0:T(8,128)} custom-call(bf16[4096,512]{1,0:T(8,128)(2,1)} %refs_0_.9, f32[4096,512]{1,0:T(8,128)} %get-tuple-element.95.refs_5_.refs_1_, bf16[4096,1664]{1,0:T(8,128)(2,1)} %get-tuple-element.114.refs_1_.refs_2_, f32[1,512]{1,0:T(1,128)} %bitcast.133, bf16[512,1664]{1,0:T(8,128)(2,1)} %bitcast.99, ...), custom_call_target="tpu_custom_call", output_to_operand_aliasing={{}: (5, {})} | custom-call | flops 1610612736 | bytes 10485760 | tf_op jit(solution)/shard_map/finish/pallas_call | solution.py:89
  427.1 2.6 collective-permute-start.24
  430.2 3.7 collective-permute-done.24
  (175 shorter events, 44.5 us)
Async XLA Ops:
  7.2 12.2 %copy-start.21 = (bf16[16,512]{1,0:T(8,128)(2,1)S(1)}, bf16[16,512]{1,0:T(8,128)(2,1)}, u32[]{:S(2)}) copy-start(bf16[16,512]{1,0:T(8,128)(2,1)} %param.23) | copy-start | bytes 49156
  7.2 13.0 %copy-start.14 = (f32[8,64,128]{2,1,0:T(8,128)S(1)}, f32[8,64,128]{2,1,0:T(8,128)}, u32[]{:S(2)}) copy-start(f32[8,64,128]{2,1,0:T(8,128)} %param.16) | copy-start | bytes 786436
  7.2 109.8 %all-gather.2.cloned.1.call-start = ((), (), s32[]{:S(2)}) async-start(), calls=%async_computation.1 | async-start | bytes 4866048 | tf_op jit(solution)/shard_map/all_gather | solution.py:954
  10.4 6.8 %collective-permute-start = (bf16[1,1,1,1,1,16,1664]{6,5,4,3,2,1,0:T(8,128)(2,1)S(1)}, bf16[1,1,1,1,1,16,1664]{6,5,4,3,2,1,0:T(8,128)(2,1)S(1)}, u32[]{:S(2)}, u32[]{:S(2)}) collective-permute-start(bf16[1,1,1,1,1,16,1664]{6,5,4,3,2,1,0:T(8,128)(2,1)S(1)} %bitcast.121), channel_id=1, source_target_pairs={{0,16},{4,20},{8,24},{12,28},{16,0},{20,4},{24,8},{28,12},{1,17},{... | collective-permute-start | bytes 159752 | tf_op jit(solution)/shard_map/ppermute | solution.py:792
  20.1 394.3 %reduce-scatter.2.cloned.1.call-start = ((), (), s32[]{:S(2)}) async-start(), calls=%async_computation.2 | async-start | bytes 9732096 | tf_op jit(solution)/shard_map/reduce_scatter | solution.py:1011
  20.3 4.8 %collective-permute-start.1 = (bf16[2,1,1,1,1,16,1664]{6,5,4,3,2,1,0:T(8,128)(2,1)S(1)}, bf16[2,1,1,1,1,16,1664]{6,5,4,3,2,1,0:T(8,128)(2,1)S(1)}, u32[]{:S(2)}, u32[]{:S(2)}) collective-permute-start(bf16[2,1,1,1,1,16,1664]{6,5,4,3,2,1,0:T(8,128)(2,1)S(1)} %maximum_select_fusion.7), channel_id=1, source_target_pairs={{0,8},{4,12},{8,0},{12,4},{16,24},{20,28},{24,16},{28,20},{1,9},{5... | collective-permute-start | bytes 319496 | tf_op jit(solution)/shard_map/ppermute | solution.py:792
  25.2 5.9 %collective-permute-start.2 = (bf16[2,2,1,1,1,16,1664]{6,5,4,3,2,1,0:T(8,128)(2,1)S(1)}, bf16[2,2,1,1,1,16,1664]{6,5,4,3,2,1,0:T(8,128)(2,1)S(1)}, u32[]{:S(2)}, u32[]{:S(2)}) collective-permute-start(bf16[2,2,1,1,1,16,1664]{6,5,4,3,2,1,0:T(8,128)(2,1)S(1)} %maximum_select_fusion.5), channel_id=1, source_target_pairs={{0,4},{4,0},{8,12},{12,8},{16,20},{20,16},{24,28},{28,24},{1,5},{5... | collective-permute-start | bytes 638984 | tf_op jit(solution)/shard_map/ppermute | solution.py:792
  31.2 8.9 %collective-permute-start.3 = (bf16[2,2,2,1,1,16,1664]{6,5,4,3,2,1,0:T(8,128)(2,1)S(1)}, bf16[2,2,2,1,1,16,1664]{6,5,4,3,2,1,0:T(8,128)(2,1)S(1)}, u32[]{:S(2)}, u32[]{:S(2)}) collective-permute-start(bf16[2,2,2,1,1,16,1664]{6,5,4,3,2,1,0:T(8,128)(2,1)S(1)} %maximum_select_fusion.3), channel_id=1, source_target_pairs={{0,2},{1,3},{2,0},{3,1},{4,6},{5,7},{6,4},{7,5},{8,10},{9,11},{10,... | collective-permute-start | bytes 1277960 | tf_op jit(solution)/shard_map/ppermute | solution.py:792
  40.2 3.4 collective-permute-start.4
  60.9 51.2 %collective-permute-start.7 = (bf16[7,528,256]{2,1,0:T(8,128)(2,1)}, bf16[7,528,256]{2,1,0:T(8,128)(2,1)}, u32[]{:S(2)}, u32[]{:S(2)}) collective-permute-start(bf16[7,528,256]{2,1,0:T(8,128)(2,1)} %get-tuple-element.71.refs_10_), channel_id=1, source_target_pairs={{0,1},{2,3},{4,5},{6,7},{8,9},{10,11},{12,13},{14,15},{16,17},{18,... | collective-permute-start | bytes 5677064 | tf_op jit(solution)/shard_map/ppermute | solution.py:883
  64.6 49.8 %collective-permute-start.8 = (bf16[7,528,256]{2,1,0:T(8,128)(2,1)}, bf16[7,528,256]{2,1,0:T(8,128)(2,1)}, u32[]{:S(2)}, u32[]{:S(2)}) collective-permute-start(bf16[7,528,256]{2,1,0:T(8,128)(2,1)} %get-tuple-element.71.refs_10_), channel_id=1, source_target_pairs={{1,2},{0,3},{5,6},{4,7},{9,10},{8,11},{13,14},{12,15},{17,18},{16,... | collective-permute-start | bytes 5677064 | tf_op jit(solution)/shard_map/ppermute | solution.py:883
  86.9 75.2 %collective-permute-start.5 = (bf16[9,528,256]{2,1,0:T(8,128)(2,1)}, bf16[9,528,256]{2,1,0:T(8,128)(2,1)S(1)}, u32[]{:S(2)}, u32[]{:S(2)}) collective-permute-start(bf16[9,528,256]{2,1,0:T(8,128)(2,1)} %get-tuple-element.73.refs_3_), channel_id=1, source_target_pairs={{0,1},{2,3},{4,5},{6,7},{8,9},{10,11},{12,13},{14,15},{16,17},{18,... | collective-permute-start | bytes 7299080 | tf_op jit(solution)/shard_map/ppermute | solution.py:883
  91.2 75.3 %collective-permute-start.6 = (bf16[9,528,256]{2,1,0:T(8,128)(2,1)}, bf16[9,528,256]{2,1,0:T(8,128)(2,1)}, u32[]{:S(2)}, u32[]{:S(2)}) collective-permute-start(bf16[9,528,256]{2,1,0:T(8,128)(2,1)} %get-tuple-element.73.refs_3_), channel_id=1, source_target_pairs={{1,2},{0,3},{5,6},{4,7},{9,10},{8,11},{13,14},{12,15},{17,18},{16,... | collective-permute-start | bytes 7299080 | tf_op jit(solution)/shard_map/ppermute | solution.py:883
  93.9 22.5 %copy-start.26 = (s32[16]{0:T(128)S(1)}, s32[16]{0:T(128)}, u32[]{:S(2)}) copy-start(s32[16]{0:T(128)} %param.15) | copy-start | bytes 196
  114.4 2.7 collective-permute-start.9
  166.5 4.7 %collective-permute-start.10 = (bf16[9,528,256]{2,1,0:T(8,128)(2,1)}, bf16[9,528,256]{2,1,0:T(8,128)(2,1)}, u32[]{:S(2)}, u32[]{:S(2)}) collective-permute-start(bf16[9,528,256]{2,1,0:T(8,128)(2,1)} %collective-permute-done.6.refs_9_), channel_id=1, source_target_pairs={{2,3},{3,2},{6,7},{7,6},{10,11},{11,10},{14,15},{15,14},{18,19},{1... | collective-permute-start | bytes 7299080 | tf_op jit(solution)/shard_map/ppermute | solution.py:883
  168.6 59.3 %collective-permute-start.13 = (bf16[7,528,256]{2,1,0:T(8,128)(2,1)}, bf16[7,528,256]{2,1,0:T(8,128)(2,1)}, u32[]{:S(2)}, u32[]{:S(2)}) collective-permute-start(bf16[7,528,256]{2,1,0:T(8,128)(2,1)} %get-tuple-element.83.refs_22_), channel_id=1, source_target_pairs={{3,2},{1,0},{7,6},{5,4},{11,10},{9,8},{15,14},{13,12},{19,18},{17,... | collective-permute-start | bytes 5677064 | tf_op jit(solution)/shard_map/ppermute | solution.py:883
  169.9 58.0 %collective-permute-start.14 = (bf16[7,528,256]{2,1,0:T(8,128)(2,1)}, bf16[7,528,256]{2,1,0:T(8,128)(2,1)}, u32[]{:S(2)}, u32[]{:S(2)}) collective-permute-start(bf16[7,528,256]{2,1,0:T(8,128)(2,1)} %get-tuple-element.83.refs_22_), channel_id=1, source_target_pairs={{2,1},{3,0},{6,5},{7,4},{10,9},{11,8},{14,13},{15,12},{18,17},{19,... | collective-permute-start | bytes 5677064 | tf_op jit(solution)/shard_map/ppermute | solution.py:883
  228.0 37.9 %collective-permute-start.16 = (bf16[7,528,256]{2,1,0:T(8,128)(2,1)}, bf16[7,528,256]{2,1,0:T(8,128)(2,1)S(1)}, u32[]{:S(2)}, u32[]{:S(2)}) collective-permute-start(bf16[7,528,256]{2,1,0:T(8,128)(2,1)} %collective-permute-done.14.refs_6_.refs_9_), channel_id=1, source_target_pairs={{1,0},{0,1},{5,4},{4,5},{9,8},{8,9},{13,12},{12,13},{17,16},{16,17... | collective-permute-start | bytes 5677064 | tf_op jit(solution)/shard_map/ppermute | solution.py:883
  232.2 33.7 %collective-permute-start.11 = (bf16[4,528,256]{2,1,0:T(8,128)(2,1)}, bf16[4,528,256]{2,1,0:T(8,128)(2,1)}, u32[]{:S(2)}, u32[]{:S(2)}) collective-permute-start(bf16[4,528,256]{2,1,0:T(8,128)(2,1)} %get-tuple-element.98.refs_7_), channel_id=1, source_target_pairs={{3,2},{1,0},{7,6},{5,4},{11,10},{9,8},{15,14},{13,12},{19,18},{17,... | collective-permute-start | bytes 3244040 | tf_op jit(solution)/shard_map/ppermute | solution.py:883
  233.5 32.4 %collective-permute-start.12 = (bf16[4,528,256]{2,1,0:T(8,128)(2,1)}, bf16[4,528,256]{2,1,0:T(8,128)(2,1)S(1)}, u32[]{:S(2)}, u32[]{:S(2)}) collective-permute-start(bf16[4,528,256]{2,1,0:T(8,128)(2,1)} %get-tuple-element.98.refs_7_), channel_id=1, source_target_pairs={{2,1},{3,0},{6,5},{7,4},{10,9},{11,8},{14,13},{15,12},{18,17},{19,... | collective-permute-start | bytes 3244040 | tf_op jit(solution)/shard_map/ppermute | solution.py:883
  267.5 42.6 %collective-permute-start.17 = (bf16[5,528,256]{2,1,0:T(8,128)(2,1)}, bf16[5,528,256]{2,1,0:T(8,128)(2,1)}, u32[]{:S(2)}, u32[]{:S(2)}) collective-permute-start(bf16[5,528,256]{2,1,0:T(8,128)(2,1)} %get-tuple-element.103.refs_12_), channel_id=1, source_target_pairs={{3,2},{1,0},{7,6},{5,4},{11,10},{9,8},{15,14},{13,12},{19,18},{17,... | collective-permute-start | bytes 4055048 | tf_op jit(solution)/shard_map/ppermute | solution.py:883
  268.8 41.4 %collective-permute-start.18 = (bf16[5,528,256]{2,1,0:T(8,128)(2,1)}, bf16[5,528,256]{2,1,0:T(8,128)(2,1)S(1)}, u32[]{:S(2)}, u32[]{:S(2)}) collective-permute-start(bf16[5,528,256]{2,1,0:T(8,128)(2,1)} %get-tuple-element.103.refs_12_), channel_id=1, source_target_pairs={{2,1},{3,0},{6,5},{7,4},{10,9},{11,8},{14,13},{15,12},{18,17},{19,... | collective-permute-start | bytes 4055048 | tf_op jit(solution)/shard_map/ppermute | solution.py:883
  270.1 45.4 %copy-start.2 = (bf16[4,528,256]{2,1,0:T(8,128)(2,1)S(1)}, bf16[4,528,256]{2,1,0:T(8,128)(2,1)}, u32[]{:S(2)}) copy-start(bf16[4,528,256]{2,1,0:T(8,128)(2,1)} %copy-done.1) | copy-start | bytes 3244036
  310.1 9.9 %collective-permute-start.19 = (bf16[5,528,256]{2,1,0:T(8,128)(2,1)S(1)}, bf16[5,528,256]{2,1,0:T(8,128)(2,1)}, u32[]{:S(2)}, u32[]{:S(2)}) collective-permute-start(bf16[5,528,256]{2,1,0:T(8,128)(2,1)S(1)} %collective-permute-done.18.refs_12_), channel_id=1, source_target_pairs={{1,0},{0,1},{5,4},{4,5},{9,8},{8,9},{13,12},{12,13},{17,16},{16,17... | collective-permute-start | bytes 4055048 | tf_op jit(solution)/shard_map/ppermute | solution.py:883
  315.5 4.6 %collective-permute-start.15 = (bf16[4,528,256]{2,1,0:T(8,128)(2,1)S(1)}, bf16[4,528,256]{2,1,0:T(8,128)(2,1)S(1)}, u32[]{:S(2)}, u32[]{:S(2)}) collective-permute-start(bf16[4,528,256]{2,1,0:T(8,128)(2,1)S(1)} %copy-done.2), channel_id=1, source_target_pairs={{1,0},{0,1},{5,4},{4,5},{9,8},{8,9},{13,12},{12,13},{17,16},{16,17... | collective-permute-start | bytes 3244040 | tf_op jit(solution)/shard_map/ppermute | solution.py:883
  321.1 50.7 %copy-start.22 = (f32[8,128]{1,0:T(8,128)S(1)}, f32[8,128]{1,0:T(8,128)}, u32[]{:S(2)}) copy-start(f32[8,128]{1,0:T(8,128)} %get-tuple-element.109) | copy-start | bytes 12292
  387.1 9.8 %collective-permute-start.20 = (bf16[272,1664]{1,0:T(8,128)(2,1)S(1)}, bf16[272,1664]{1,0:T(8,128)(2,1)S(1)}, u32[]{:S(2)}, u32[]{:S(2)}) collective-permute-start(bf16[272,1664]{1,0:T(8,128)(2,1)S(1)} %pad_maximum_fusion.refs_5_), channel_id=1, source_target_pairs={{0,1},{1,0},{2,3},{3,2},{4,5},{5,4},{6,7},{7,6},{8,9},{9,8},{10,11... | collective-permute-start | bytes 2715656 | tf_op jit(solution)/shard_map/ppermute | solution.py:792
  399.2 13.1 %collective-permute-start.21 = (bf16[144,1664]{1,0:T(8,128)(2,1)S(1)}, bf16[144,1664]{1,0:T(8,128)(2,1)S(1)}, u32[]{:S(2)}, u32[]{:S(2)}) collective-permute-start(bf16[144,1664]{1,0:T(8,128)(2,1)S(1)} %pad_maximum_fusion.1.refs_6_), channel_id=1, source_target_pairs={{0,2},{1,3},{2,0},{3,1},{4,6},{5,7},{6,4},{7,5},{8,10},{9,11},{10,... | collective-permute-start | bytes 1437704 | tf_op jit(solution)/shard_map/ppermute | solution.py:792
  412.7 8.7 %collective-permute-start.22 = (bf16[80,1664]{1,0:T(8,128)(2,1)S(1)}, bf16[80,1664]{1,0:T(8,128)(2,1)S(1)}, u32[]{:S(2)}, u32[]{:S(2)}) collective-permute-start(bf16[80,1664]{1,0:T(8,128)(2,1)S(1)} %pad_maximum_fusion.3.refs_6_), channel_id=1, source_target_pairs={{0,4},{4,0},{8,12},{12,8},{16,20},{20,16},{24,28},{28,24},{1,5},{5... | collective-permute-start | bytes 798728 | tf_op jit(solution)/shard_map/ppermute | solution.py:792
  421.6 5.3 %collective-permute-start.23 = (bf16[48,1664]{1,0:T(8,128)(2,1)S(1)}, bf16[48,1664]{1,0:T(8,128)(2,1)S(1)}, u32[]{:S(2)}, u32[]{:S(2)}) collective-permute-start(bf16[48,1664]{1,0:T(8,128)(2,1)S(1)} %pad_maximum_fusion.5), channel_id=1, source_target_pairs={{0,8},{4,12},{8,0},{12,4},{16,24},{20,28},{24,16},{28,20},{1,9},{5... | collective-permute-start | bytes 479240 | tf_op jit(solution)/shard_map/ppermute | solution.py:792
  427.1 6.8 %collective-permute-start.24 = (bf16[32,1664]{1,0:T(8,128)(2,1)S(1)}, bf16[32,1664]{1,0:T(8,128)(2,1)S(1)}, u32[]{:S(2)}, u32[]{:S(2)}) collective-permute-start(bf16[32,1664]{1,0:T(8,128)(2,1)S(1)} %pad_maximum_fusion.7), channel_id=1, source_target_pairs={{0,16},{4,20},{8,24},{12,28},{16,0},{20,4},{24,8},{28,12},{1,17},{... | collective-permute-start | bytes 319496 | tf_op jit(solution)/shard_map/ppermute | solution.py:792
  (22 other events, 124.1 us)
Sparse Core Ops, SparseCore 0:
  20.2 65.2 all-gather.1
  266.1 139.5 reduce-scatter.1
